TPU v7x, 512 devices: a whole 4x8x8 slice. The times are simulated.
512 devices in a mesh: ctx: 16 (over x, y_hi, core), exp: 32 (over z, y_lo).
Axes of the slice: x: 4, y: 8 (y_hi: 2, y_lo: 4; y = y_hi * 4 + y_lo), z: 8, core: 2. Of those that a mesh axis runs over, the one named last changes fastest.
Arguments:
- queries: bfloat16 [32, 2048, 2048], P('exp', 'ctx'), may hold values from -64 to 64
- key_rows: bfloat16 [32, 2048, 256], P('exp', 'ctx'), may hold values from -6 to 6
- values: bfloat16 [32, 2048, 256], P('exp', 'ctx'), may hold values from -6 to 6
- residual: bfloat16 [32, 2048, 2048], P('exp', 'ctx'), may hold values from -6 to 6
- seg_lengths: int32 [32, 32], P('exp'), may hold values from 1 to 512, 2048 in all within a row
- seg_parent: int32 [32, 32], P('exp'), may hold values from 0 to 30, as said below
- ln_gain: float32 [2048], replicated, may hold values from 0.25 to 1.75
- w_gate: bfloat16 [32, 2048, 384], P('exp', 'ctx'), may hold values from -0.125 to 0.125
- w_up: bfloat16 [32, 2048, 384], P('exp', 'ctx'), may hold values from -0.125 to 0.125
- w_down: bfloat16 [32, 384, 2048], P('exp', None, 'ctx'), may hold values from -0.3125 to 0.3125
- expert_ids: int32 [32, 2048, 8], P('exp', 'ctx'), may hold values from 0 to 127, all different within a row; in each aligned block of 128 rows (0 to 127, 128 to 255, ..., all dimensions but the last counted through in order) at most 10 rows name the same one
- gate_weights: float32 [32, 2048, 8], P('exp', 'ctx'), may hold values from 0.2 to 1
- cotangent: bfloat16 [32, 2048, 2048], P('exp', 'ctx'), may hold values from -6 to 6
Outputs:
- mixed_out: bfloat16 [32, 2048, 2048], P('exp', 'ctx')
- stream_grad: float32 [32, 2048, 2048], P('exp', 'ctx')
Inputs may be any that keep to these rules, and one draw needn't show every extreme that they name: `expert_ids`: in each aligned block of 128 rows (the rows of one device) no id is named by more than 10 rows. seg_parent[b, 0] = 0, and seg_parent[b, s] < s for every segment s >= 1. `seg_lengths`: each slab's lengths sum to 2048.
All inputs are finite; a program needn't handle non-finite values.
Results may differ from a plain program's by a relative error of at most 0.0095.
Values may be sent and summed in bfloat16 or wider, within the bound.
No kernel may reach another device: no remote copies, remote signals or barrier semaphores. Data moves between devices by JAX's collectives and lax.ppermute only.
A program may use at most 64 MiB of HBM per device.

v0:
```python
import math

import jax
import jax.numpy as jnp
from jax import lax
from jax.sharding import PartitionSpec as P

HEAD_DIM = 128
TOPK = 8
CAP = 10


def ancestry(parent):
    seg_count = parent.shape[0]
    index = jnp.arange(seg_count, dtype=jnp.int32)
    linked = (parent[:, None] == index[None, :]) | (index[:, None] == index[None, :])
    reached = linked.astype(jnp.float32)
    for sweep in range(max(1, (seg_count - 1).bit_length())):
        reached = jnp.minimum(jnp.dot(reached, reached, precision=lax.Precision.HIGHEST), 1.0)
    return reached


def segment_onehot(position, lengths):
    starts = jnp.cumsum(lengths) - lengths
    finish = starts + lengths
    inside = (position[:, None] >= starts[None, :]) & (position[:, None] < finish[None, :])
    return inside.astype(jnp.float32)


def expert_forward(rows_in, weights_now):
    weight_gate, weight_up, weight_down = weights_now
    flat_rows = rows_in.reshape(-1, rows_in.shape[-1])
    gate_proj = jnp.dot(flat_rows, weight_gate, preferred_element_type=jnp.float32)
    up_proj = jnp.dot(flat_rows, weight_up, preferred_element_type=jnp.float32)
    sigmoid_gate = jax.nn.sigmoid(gate_proj)
    activated = (gate_proj * sigmoid_gate * up_proj).astype(jnp.bfloat16)
    expert_out = jnp.dot(activated, weight_down, preferred_element_type=jnp.float32).astype(
        jnp.bfloat16
    )
    return (expert_out.reshape(rows_in.shape), (gate_proj, up_proj, sigmoid_gate))


def expert_backward(rows_grad, saved, weights_now):
    weight_gate, weight_up, weight_down = weights_now
    gate_proj, up_proj, sigmoid_gate = saved
    flat_rows = rows_grad.reshape(-1, rows_grad.shape[-1])
    contract = (((1,), (1,)), ((), ()))
    back_grad = lax.dot_general(
        flat_rows, weight_down, contract, preferred_element_type=jnp.float32
    )
    d_gate = (back_grad * up_proj * sigmoid_gate * (1.0 + gate_proj * (1.0 - sigmoid_gate))).astype(
        jnp.bfloat16
    )
    d_up = (back_grad * gate_proj * sigmoid_gate).astype(jnp.bfloat16)
    expert_grad = lax.dot_general(
        d_gate, weight_gate, contract, preferred_element_type=jnp.float32
    ) + lax.dot_general(d_up, weight_up, contract, preferred_element_type=jnp.float32)
    return expert_grad.astype(jnp.bfloat16).reshape(rows_grad.shape)


def on_device(
    queries,
    key_rows,
    values,
    residual,
    seg_lengths,
    seg_parent,
    ln_gain,
    w_gate,
    w_up,
    w_down,
    expert_ids,
    gate_weights,
    cotangent,
):
    groups = lax.axis_size("exp")
    rows_here = queries.shape[1]
    model_width = residual.shape[2]
    kv_count = key_rows.shape[2] // HEAD_DIM
    head_count = queries.shape[2] // HEAD_DIM
    group_size = head_count // kv_count
    score_scale = HEAD_DIM ** (-0.5)
    lengths = seg_lengths[0]
    reach_table = ancestry(seg_parent[0])
    first_row = lax.axis_index("ctx") * rows_here
    query_pos = first_row + jnp.arange(rows_here, dtype=jnp.int32)
    query_reach = jnp.dot(
        segment_onehot(query_pos, lengths), reach_table, precision=lax.Precision.HIGHEST
    )
    query_heads = queries[0].reshape(rows_here, kv_count, group_size, HEAD_DIM)
    key_slab, value_slab = (
        lax.all_gather(key_rows, "ctx", axis=1, tiled=True),
        lax.all_gather(values, "ctx", axis=1, tiled=True),
    )
    key_all = key_slab[0]
    value_all = value_slab[0]
    key_count = key_all.shape[0]
    block_rows = math.gcd(key_count, 512)

    def attend_block(block_number, running):
        block_start = (block_number * block_rows).astype(jnp.int32)
        key_block = lax.dynamic_slice_in_dim(key_all, block_start, block_rows, 0).reshape(
            block_rows, kv_count, HEAD_DIM
        )
        value_block = lax.dynamic_slice_in_dim(value_all, block_start, block_rows, 0).reshape(
            block_rows, kv_count, HEAD_DIM
        )
        key_pos = block_start + jnp.arange(block_rows, dtype=jnp.int32)
        linked = jnp.dot(
            query_reach, segment_onehot(key_pos, lengths).T, precision=lax.Precision.HIGHEST
        )
        visible = (linked > 0.5) & (key_pos[None, :] <= query_pos[:, None])
        running_max, denominator, weighted = running
        scores = (
            jnp.einsum("tkgd,skd->kgts", query_heads, key_block, preferred_element_type=jnp.float32)
            * score_scale
        )
        new_max = jnp.maximum(
            running_max, jnp.max(jnp.where(visible[None, None], scores, -1e30), -1)
        )
        weights_now = jnp.where(visible[None, None], jnp.exp(scores - new_max[..., None]), 0.0)
        shrink = jnp.exp(running_max - new_max)
        weighted = weighted * shrink[..., None] + jnp.einsum(
            "kgts,skd->kgtd",
            weights_now.astype(jnp.bfloat16),
            value_block,
            preferred_element_type=jnp.float32,
        )
        denominator = denominator * shrink + jnp.sum(weights_now, -1)
        return (new_max, denominator, weighted)

    initial = (
        jnp.full((kv_count, group_size, rows_here), -1e30, jnp.float32),
        jnp.zeros((kv_count, group_size, rows_here), jnp.float32),
        jnp.zeros((kv_count, group_size, rows_here, HEAD_DIM), jnp.float32),
    )
    running_max, denominator, weighted = lax.fori_loop(
        0, key_count // block_rows, attend_block, initial
    )
    attended = jnp.transpose(weighted / denominator[..., None], (2, 0, 1, 3))
    attended = attended.reshape(rows_here, model_width).astype(jnp.bfloat16)
    stream = residual[0].astype(jnp.float32) + attended.astype(jnp.float32)
    scale_back = lax.rsqrt(jnp.mean(stream * stream, -1, keepdims=True) + 1e-06)
    normed = (stream * scale_back * ln_gain).astype(jnp.bfloat16)
    route_ids = expert_ids[0].reshape(-1)
    route_count = route_ids.shape[0]
    room = groups * CAP
    in_window = route_ids < groups
    onehot = (route_ids[:, None] == jnp.arange(groups, dtype=jnp.int32)[None, :]).astype(jnp.int32)
    earlier = jnp.sum((jnp.cumsum(onehot, 0) - onehot) * onehot, 1)
    slot_index = jnp.where(in_window, route_ids * CAP + earlier, room)
    token_index = jnp.arange(route_count, dtype=jnp.int32) // TOPK
    source = jnp.zeros((room,), jnp.int32).at[slot_index].set(token_index, mode="drop")
    filled = jnp.zeros((room,), jnp.bool_).at[slot_index].set(True, mode="drop")
    take = jnp.minimum(slot_index, room - 1).reshape(rows_here, TOPK)
    factor = jnp.where(in_window, gate_weights[0].reshape(-1), 0.0).reshape(rows_here, TOPK)

    def gather_rows(table):
        return jnp.where(filled[:, None], table[source], 0).reshape(groups, CAP, model_width)

    def combine(returned):
        flat_rows = returned.reshape(room, model_width)
        summed = jnp.zeros((rows_here, model_width), jnp.float32)
        for chosen in range(TOPK):
            summed = summed + factor[:, chosen, None] * flat_rows[take[:, chosen]].astype(
                jnp.float32
            )
        return summed

    gathered = (
        lax.all_gather(w_gate, "ctx", axis=1, tiled=True),
        lax.all_gather(w_up, "ctx", axis=1, tiled=True),
        lax.all_gather(w_down, "ctx", axis=2, tiled=True),
    )
    weights_now = (gathered[0][0], gathered[1][0], gathered[2][0])
    send_input = gather_rows(normed)
    send_grad = gather_rows(cotangent[0])
    arrived_in = lax.all_to_all(send_input, "exp", split_axis=0, concat_axis=0, tiled=True)
    expert_out, saved = expert_forward(arrived_in, weights_now)
    back_out = lax.all_to_all(expert_out, "exp", split_axis=0, concat_axis=0, tiled=True)
    again = (
        lax.all_gather(w_gate, "ctx", axis=1, tiled=True),
        lax.all_gather(w_up, "ctx", axis=1, tiled=True),
        lax.all_gather(w_down, "ctx", axis=2, tiled=True),
    )
    weights_now = (again[0][0], again[1][0], again[2][0])
    arrived_grad = lax.all_to_all(send_grad, "exp", split_axis=0, concat_axis=0, tiled=True)
    grad_in = expert_backward(arrived_grad, saved, weights_now)
    back_grad = lax.all_to_all(grad_in, "exp", split_axis=0, concat_axis=0, tiled=True)
    mixed_out = (stream + combine(back_out)).astype(jnp.bfloat16)
    grad_normed = combine(back_grad)
    gain_grad = ln_gain * grad_normed
    inner = jnp.mean(stream * gain_grad, -1, keepdims=True)
    stream_grad = (
        cotangent[0].astype(jnp.float32) + scale_back * gain_grad - stream * scale_back**3 * inner
    )
    return (mixed_out[None], stream_grad[None])


def solution(mesh):
    placed = (
        P("exp", "ctx", None),
        P("exp", "ctx", None),
        P("exp", "ctx", None),
        P("exp", "ctx", None),
        P("exp", None),
        P("exp", None),
        P(),
        P("exp", "ctx", None),
        P("exp", "ctx", None),
        P("exp", None, "ctx"),
        P("exp", "ctx", None),
        P("exp", "ctx", None),
        P("exp", "ctx", None),
    )
    return jax.shard_map(
        on_device,
        mesh=mesh,
        in_specs=placed,
        out_specs=(P("exp", "ctx", None), P("exp", "ctx", None)),
        check_vma=False,
    )
```

profile of v0, /device:TPU:56, one launch (start us, length us, event | category | flops | bytes accessed | tf_op | source)
XLA Modules:
  0.0 504.6 jit_solution(11859694236968934481)
XLA Ops:
  7.2 1.6 copy.44
  8.9 1.6 copy.46
  16.6 9.0 %reduce-window.21 = s32[32,8,128]{2,1,0:T(8,128)S(1)} reduce-window(s32[32,8,128]{2,1,0:T(8,128)S(1)} %fusion.83, s32[]{:T(128)} %constant.129.clone.1), window={size=1x1x128 pad=0_0x0_0x127_0}, to_apply=%region_5.6 | reduce-window | flops 4161536 | bytes 262148 | tf_op jit(solution)/shard_map/reduce-window.1
  26.5 4.3 scatter_custom_fusion.1
  30.9 2.4 gather_fusion.9
  33.3 1.5 gather.69
  34.9 4.5 scatter_custom_fusion
  40.4 31.9 %all-gather.6.cloned.1.call-done = bf16[1,2048,256]{1,2,0:T(8,128)(2,1)} async-done(((bf16[1,128,256]{1,2,0:T(8,128)(2,1)}), bf16[1,2048,256]{1,2,0:T(8,128)(2,1)}) %all-gather.6.cloned.1.call-update) | async-done | bytes 1048592 | tf_op jit(solution)/shard_map/all_gather | solution.py:92
  72.2 60.4 %all-gather.8.cloned.1.call-done = bf16[1,2048,256]{1,2,0:T(8,128)(2,1)} async-done(((bf16[1,128,256]{1,2,0:T(8,128)(2,1)}), bf16[1,2048,256]{1,2,0:T(8,128)(2,1)}) %all-gather.8.cloned.1.call-update) | async-done | bytes 1048592 | tf_op jit(solution)/shard_map/all_gather | solution.py:93
  132.6 41.3 %while.20 = (s32[]{:T(128)}, f32[2,8,128]{2,1,0:T(8,128)S(1)}, f32[2,8,128]{2,1,0:T(8,128)S(1)}, f32[2,8,128,128]{3,2,1,0:T(8,128)}, s32[1,32]{1,0:T(1,128)S(1)}...) while((s32[]{:T(128)}, f32[2,8,128]{2,1,0:T(8,128)S(1)}, ...), condition=%wide.region_4.5_spmd.clone, body=%wide.region_1.4_spmd.clone.sunk | while | flops 574614144 | bytes 42358308 | solution.py:137
  134.0 2.9 fusion.148
  136.9 3.2 fusion.149
  140.4 1.5 fusion.151
  144.3 2.9 fusion.148
  147.3 3.2 fusion.149
  150.7 1.5 fusion.151
  154.7 2.9 fusion.148
  157.6 3.2 fusion.149
  161.0 1.5 fusion.151
  165.0 2.9 fusion.148
  167.9 3.2 fusion.149
  171.4 1.5 fusion.151
  173.9 1.6 convert_bitcast_fusion.9
  178.7 2.6 gather_fusion
  181.3 1.6 gather.59
  182.8 3.9 broadcast_select_fusion
  186.7 64.2 %all_to_all.20 = bf16[32,10,2048]{2,1,0:T(8,128)(2,1)} all-to-all(bf16[32,10,2048]{2,1,0:T(8,128)(2,1)S(1)} %get-tuple-element.362), channel_id=1, replica_groups=mesh['ctx'=16,'exp'=32] {'exp'}, dimensions={0} | all-to-all | bytes 2621440 | tf_op jit(solution)/shard_map/all_to_all | solution.py:178
  251.0 11.4 %all-to-all-start.2 = ((bf16[32,10,2048]{2,1,0:T(8,128)(2,1)}), bf16[32,10,2048]{2,1,0:T(8,128)(2,1)}, u32[]{:S(2)}, u32[]{:S(2)}) async-start(bf16[32,10,2048]{2,1,0:T(8,128)(2,1)} %get-tuple-element.361), calls=%async_computation.2 | async-start | bytes 4194304 | tf_op jit(solution)/shard_map/all_to_all | solution.py:187
  263.0 2.5 reshape.958
  265.5 44.6 %all-to-all-done.2 = bf16[32,10,2048]{2,1,0:T(8,128)(2,1)} async-done(((bf16[32,10,2048]{2,1,0:T(8,128)(2,1)}), bf16[32,10,2048]{2,1,0:T(8,128)(2,1)}, u32[]{:S(2)}, u32[]{:S(2)}) %all-to-all-start.2) | async-done | bytes 1310752 | tf_op jit(solution)/shard_map/all_to_all | solution.py:187
  310.1 3.6 reshape.961
  313.7 2.2 fusion.36
  315.9 3.0 fusion.32
  319.0 9.2 %all-gather.14.cloned.1.call-done = bf16[1,384,2048]{2,1,0:T(8,128)(2,1)} async-done(((bf16[1,384,128]{2,1,0:T(8,128)(2,1)}), bf16[1,384,2048]{2,1,0:T(8,128)(2,1)}) %all-gather.14.cloned.1.call-update) | async-done | bytes 1572880 | tf_op jit(solution)/shard_map/all_gather | solution.py:173
  328.1 2.8 fusion.28
  333.3 1.6 reshape.962
  334.9 13.6 %all-to-all-start.3 = ((bf16[32,10,2048]{2,1,0:T(8,128)(2,1)}), bf16[32,10,2048]{2,1,0:T(8,128)(2,1)}, u32[]{:S(2)}, u32[]{:S(2)}) async-start(bf16[32,10,2048]{2,1,0:T(8,128)(2,1)} %reshape.962), calls=%async_computation.3 | async-start | bytes 4194304 | tf_op jit(solution)/shard_map/all_to_all | solution.py:189
  348.5 2.4 convolution_convert_fusion
  350.9 1.6 reshape.959
  352.5 47.4 %all-to-all-done.3 = bf16[32,10,2048]{2,1,0:T(8,128)(2,1)} async-done(((bf16[32,10,2048]{2,1,0:T(8,128)(2,1)}), bf16[32,10,2048]{2,1,0:T(8,128)(2,1)}, u32[]{:S(2)}, u32[]{:S(2)}) %all-to-all-start.3) | async-done | bytes 1310752 | tf_op jit(solution)/shard_map/all_to_all | solution.py:189
  399.9 11.6 %all-to-all-start.1 = ((bf16[32,10,2048]{2,1,0:T(8,128)(2,1)}), bf16[32,10,2048]{2,1,0:T(8,128)(2,1)}, u32[]{:S(2)}, u32[]{:S(2)}) async-start(bf16[32,10,2048]{2,1,0:T(8,128)(2,1)} %reshape.959), calls=%async_computation.1 | async-start | bytes 4194304 | tf_op jit(solution)/shard_map/all_to_all | solution.py:180
  412.5 1.1 reshape.964
  413.7 2.5 reshape.963
  416.2 1.7 gather_fusion.11
  417.9 1.7 gather_fusion.10
  419.6 43.5 %all-to-all-done.1 = bf16[32,10,2048]{2,1,0:T(8,128)(2,1)} async-done(((bf16[32,10,2048]{2,1,0:T(8,128)(2,1)}), bf16[32,10,2048]{2,1,0:T(8,128)(2,1)}, u32[]{:S(2)}, u32[]{:S(2)}) %all-to-all-start.1) | async-done | bytes 1310752 | tf_op jit(solution)/shard_map/all_to_all | solution.py:180
  463.1 2.5 reshape.960
  465.6 1.7 gather_fusion.1
  467.4 1.7 gather_fusion.2
  469.1 1.7 gather_fusion.12
  470.8 1.7 gather_fusion.3
  472.6 1.7 gather_fusion.13
  474.3 1.7 gather_fusion.4
  476.0 1.7 gather_fusion.14
  477.8 1.7 gather_fusion.5
  479.5 1.7 gather_fusion.15
  481.2 1.7 gather_fusion.6
  482.9 1.8 gather_fusion.16
  484.7 1.7 gather_fusion.7
  486.4 1.8 gather_fusion.17
  488.2 1.7 gather_fusion.8
  490.0 3.6 fusion.76
  494.0 2.2 fusion.50
  496.3 1.8 fusion.69
  (190 shorter events, 25.6 us)
Async XLA Ops:
  7.2 8.9 %copy-start.27 = (bf16[1,128,2048]{2,1,0:T(8,128)(2,1)S(1)}, bf16[1,128,2048]{2,1,0:T(8,128)(2,1)}, u32[]{:S(2)}) copy-start(bf16[1,128,2048]{2,1,0:T(8,128)(2,1)} %param.15) | copy-start | bytes 1572868
  7.2 65.0 %all-gather.6.cloned.1.call-start = ((), (), s32[]{:S(2)}) async-start(), calls=%async_computation.4 | async-start | bytes 1114112 | tf_op jit(solution)/shard_map/all_gather | solution.py:92
  8.9 123.7 %all-gather.8.cloned.1.call-start = ((), (), s32[]{:S(2)}) async-start(), calls=%async_computation.5 | async-start | bytes 1114112 | tf_op jit(solution)/shard_map/all_gather | solution.py:93
  10.5 303.1 %all-gather.10.cloned.1.call-start = ((), (), s32[]{:S(2)}) async-start(), calls=%async_computation.6 | async-start | bytes 1671168 | tf_op jit(solution)/shard_map/all_gather | solution.py:171
  11.3 304.7 %all-gather.12.cloned.1.call-start = ((), (), s32[]{:S(2)}) async-start(), calls=%async_computation.7 | async-start | bytes 1671168 | tf_op jit(solution)/shard_map/all_gather | solution.py:172
  16.0 10.1 %copy-start.35 = (f32[1,128,8]{1,2,0:T(8,128)S(1)}, f32[1,128,8]{1,2,0:T(8,128)}, u32[]{:S(2)}) copy-start(f32[1,128,8]{1,2,0:T(8,128)} %param.26) | copy-start | bytes 12292
  16.3 14.5 %copy-start.1 = (bf16[1,128,2048]{2,1,0:T(8,128)(2,1)S(1)}, bf16[1,128,2048]{2,1,0:T(8,128)(2,1)}, u32[]{:S(2)}) copy-start(bf16[1,128,2048]{2,1,0:T(8,128)(2,1)} %param.27) | copy-start | bytes 1572868
  26.5 6.8 %copy-start.31 = (s32[1024]{0:T(1024)}, s32[1024]{0:T(1024)S(1)}, u32[]{:S(2)}) copy-start(s32[1024]{0:T(1024)S(1)} %fusion.82) | copy-start | bytes 12292
  30.9 2.5 copy-start.33
  134.0 6.1 %copy-start.25 = (f32[2,8,128,128]{3,2,1,0:T(8,128)S(1)}, f32[2,8,128,128]{3,2,1,0:T(8,128)}, u32[]{:S(2)}) copy-start(f32[2,8,128,128]{3,2,1,0:T(8,128)} %get-tuple-element.470) | copy-start | bytes 3145732 | tf_op jit(solution)/shard_map/while
  136.9 3.4 copy-start
  141.9 1.0 copy-start.26
  144.3 6.1 %copy-start.25 = (f32[2,8,128,128]{3,2,1,0:T(8,128)S(1)}, f32[2,8,128,128]{3,2,1,0:T(8,128)}, u32[]{:S(2)}) copy-start(f32[2,8,128,128]{3,2,1,0:T(8,128)} %get-tuple-element.470) | copy-start | bytes 3145732 | tf_op jit(solution)/shard_map/while
  147.3 3.4 copy-start
  152.2 1.0 copy-start.26
  154.6 6.1 %copy-start.25 = (f32[2,8,128,128]{3,2,1,0:T(8,128)S(1)}, f32[2,8,128,128]{3,2,1,0:T(8,128)}, u32[]{:S(2)}) copy-start(f32[2,8,128,128]{3,2,1,0:T(8,128)} %get-tuple-element.470) | copy-start | bytes 3145732 | tf_op jit(solution)/shard_map/while
  157.6 3.5 copy-start
  162.6 1.0 copy-start.26
  165.0 6.1 %copy-start.25 = (f32[2,8,128,128]{3,2,1,0:T(8,128)S(1)}, f32[2,8,128,128]{3,2,1,0:T(8,128)}, u32[]{:S(2)}) copy-start(f32[2,8,128,128]{3,2,1,0:T(8,128)} %get-tuple-element.470) | copy-start | bytes 3145732 | tf_op jit(solution)/shard_map/while
  167.9 3.4 copy-start
  172.9 1.0 copy-start.26
  175.4 1.0 copy-start.4
  175.5 2.7 copy-start.29
  176.1 236.4 %copy-start.2 = (f32[128,2,8,128]{3,2,1,0:T(8,128)}, f32[128,2,8,128]{3,2,1,0:T(8,128)S(1)}, u32[]{:S(2)}) copy-start(f32[128,2,8,128]{3,2,1,0:T(8,128)S(1)} %copy.50) | copy-start | bytes 3145732
  177.6 0.5 copy-start.36
  181.2 1.6 copy-start.34
  251.0 59.1 %all-to-all-start.2 = ((bf16[32,10,2048]{2,1,0:T(8,128)(2,1)}), bf16[32,10,2048]{2,1,0:T(8,128)(2,1)}, u32[]{:S(2)}, u32[]{:S(2)}) async-start(bf16[32,10,2048]{2,1,0:T(8,128)(2,1)} %get-tuple-element.361), calls=%async_computation.2 | async-start | bytes 4194304 | tf_op jit(solution)/shard_map/all_to_all | solution.py:187
  262.4 65.7 %all-gather.14.cloned.1.call-start = ((), (), s32[]{:S(2)}) async-start(), calls=%async_computation.8 | async-start | bytes 1671168 | tf_op jit(solution)/shard_map/all_gather | solution.py:173
  319.0 12.0 %copy-start.28 = (f32[320,384]{1,0:T(8,128)S(1)}, f32[320,384]{1,0:T(8,128)}, u32[]{:S(2)}) copy-start(f32[320,384]{1,0:T(8,128)} %fusion.32) | copy-start | bytes 1474564
  328.1 2.8 copy-start.23
  330.9 1.4 copy-start.24
  334.9 65.0 %all-to-all-start.3 = ((bf16[32,10,2048]{2,1,0:T(8,128)(2,1)}), bf16[32,10,2048]{2,1,0:T(8,128)(2,1)}, u32[]{:S(2)}, u32[]{:S(2)}) async-start(bf16[32,10,2048]{2,1,0:T(8,128)(2,1)} %reshape.962), calls=%async_computation.3 | async-start | bytes 4194304 | tf_op jit(solution)/shard_map/all_to_all | solution.py:189
  352.5 59.1 %copy-start.32 = (s32[1024]{0:T(1024)S(1)}, s32[1024]{0:T(1024)}, u32[]{:S(2)}) copy-start(s32[1024]{0:T(1024)} %copy-done.31) | copy-start | bytes 12292
  399.9 63.2 %all-to-all-start.1 = ((bf16[32,10,2048]{2,1,0:T(8,128)(2,1)}), bf16[32,10,2048]{2,1,0:T(8,128)(2,1)}, u32[]{:S(2)}, u32[]{:S(2)}) async-start(bf16[32,10,2048]{2,1,0:T(8,128)(2,1)} %reshape.959), calls=%async_computation.1 | async-start | bytes 4194304 | tf_op jit(solution)/shard_map/all_to_all | solution.py:180
  488.2 1.7 copy-start.3
  488.2 1.7 copy-start.30
  489.9 3.8 copy-start.5
  489.9 3.8 copy-start.6
  489.9 3.8 copy-start.7
  489.9 3.8 copy-start.8
  489.9 3.8 copy-start.9
  489.9 3.8 copy-start.10
  490.0 3.8 copy-start.11
  490.0 3.8 copy-start.12
  490.0 3.8 copy-start.13
  490.0 4.0 copy-start.14
  490.0 4.0 copy-start.37
  490.0 4.0 copy-start.38
  494.0 2.3 copy-start.15
  494.0 2.3 copy-start.16
  494.0 2.3 copy-start.17
  494.0 2.2 copy-start.18
  494.0 2.2 copy-start.19
  494.0 2.2 copy-start.20
  494.0 2.2 copy-start.21
  494.0 2.2 copy-start.22
Sparse Core Ops, SparseCore 0:
  11.7 60.4 all-gather.5
  75.3 57.1 all-gather.7
  135.8 60.9 all-gather.9
  200.0 62.2 all-gather.11
  266.1 62.0 all-gather.13
where the time goes:
time: 506 us; the launch traced here: 505 us
  waiting for transfers between devices  239 us (47%)
  local copies, waits for them, and re-layouts  78.8 us (16%)
  blocking collectives  64.2 us (13%)
  other arithmetic  38.1 us (8%)
  starting transfers between devices  36.8 us (7%)
  matrix products  33.2 us (7%)
  between operations  14.5 us (3%)
    all_to_all x1, blocking collectives, on_device(): lax.all_to_all(send_input, 'exp', split_axis=0, concat_axis=0, tiled=True)  64.2 us
    all_gather x1, waiting for transfers between devices, on_device(): lax.all_gather(values, 'ctx', axis=1, tiled=True)  60.4 us
    all_to_all x1, waiting for transfers between devices, on_device(): lax.all_to_all(grad_in, 'exp', split_axis=0, concat_axis=0, tiled=True)  47.4 us
    all_to_all x1, waiting for transfers between devices, on_device(): lax.all_to_all(send_grad, 'exp', split_axis=0, concat_axis=0, tiled=True)  44.6 us
    all_to_all x1, waiting for transfers between devices, on_device(): lax.all_to_all(expert_out, 'exp', split_axis=0, concat_axis=0, tiled=True)  43.5 us
    all_gather x1, waiting for transfers between devices, on_device(): lax.all_gather(key_rows, 'ctx', axis=1, tiled=True)  31.9 us
    gather x16, local copies, waits for them, and re-layouts, combine(): flat_rows[take[:, chosen]].astype(jnp.float32)  27.7 us
    all_to_all x1, starting transfers between devices, on_device(): lax.all_to_all(grad_in, 'exp', split_axis=0, concat_axis=0, tiled=True)  13.6 us
  transfers between devices with their start and end apart: 8, of which 6 were waited for; matrix products, arithmetic and copies ran while one was open for 20% of the time, Pallas kernels for 0%

commit v1 on v0

v1 whole, which is shorter than its diff:
```python
import functools
import math

import jax
import jax.numpy as jnp
from jax import lax
from jax.experimental import pallas as pl
from jax.experimental.pallas import tpu as pltpu
from jax.sharding import PartitionSpec as P

HEAD_DIM = 128
TOPK = 8
CAP = 10
BLOCK = 8
NO_SLOT = 512.0
HIDDEN = -1e30
F32 = jnp.float32
BF16 = jnp.bfloat16
NT = (((1,), (1,)), ((), ()))


def iota(shape, dim):
    return lax.broadcasted_iota(jnp.int32, shape, dim)


def dot(a, b):
    return jnp.dot(a, b, preferred_element_type=F32)


def dot_nt(a, b):
    return lax.dot_general(a, b, NT, preferred_element_type=F32)


def call(body, outs, scratch=(), flops=0, moved=0):
    return pl.pallas_call(
        body,
        out_shape=outs,
        scratch_shapes=list(scratch),
        compiler_params=pltpu.CompilerParams(vmem_limit_bytes=48 << 20),
        cost_estimate=pl.CostEstimate(flops=flops, bytes_accessed=moved, transcendentals=0),
    )


def slot_keys(ids_t, groups):
    tokens = ids_t.shape[1]
    group = iota((groups, tokens), 0)
    named = jnp.zeros((groups, tokens), F32)
    for route in range(ids_t.shape[0]):
        named = named + jnp.where(ids_t[route : route + 1, :] == group, 1.0, 0.0)
    before = (iota((tokens, tokens), 0) < iota((tokens, tokens), 1)).astype(F32)
    rank = dot(named.astype(BF16), before.astype(BF16))
    key = jnp.where(named > 0.5, rank, NO_SLOT).astype(BF16)
    rows = groups * BLOCK
    spread = (iota((rows, groups), 0) // BLOCK == iota((rows, groups), 1)).astype(F32)
    return dot(spread.astype(BF16), key)


def dispatch(rows, keys, out_ref):
    place = iota(keys.shape, 0)
    width = rows.shape[1]
    part = width // 4
    pick = jnp.where(keys == (place % BLOCK).astype(F32), 1.0, 0.0).astype(BF16)
    out_ref[:, :width] = dot(pick, rows).astype(BF16)
    late = keys == (BLOCK + (place % BLOCK) // 4).astype(F32)
    tail = jnp.zeros((keys.shape[0], part), F32)
    for k in range(4):
        pick = jnp.where(late & (place % 4 == k), 1.0, 0.0).astype(BF16)
        tail = tail + dot(pick, rows[:, k * part : (k + 1) * part])
    out_ref[:, width:] = tail.astype(BF16)


def pack_body(key_ref, value_ref, gate_ref, up_ref, down_ref, kv_ref, w_ref):
    kv_ref[:, :256] = key_ref[...]
    kv_ref[:, 256:] = value_ref[...]
    w_ref[:, :384] = gate_ref[...]
    w_ref[:, 384:768] = up_ref[...]
    w_ref[:, 768:] = down_ref[...].T


def prepare_body(groups, me_ref, cot_ref, ids_t_ref, len_row_ref, len_col_ref, parent_ref, bias_ref, send_ref):
    segs = len_row_ref.shape[1]
    rows = cot_ref.shape[0]
    low, high = iota((segs, segs), 0), iota((segs, segs), 1)
    start_col = jnp.sum(jnp.where(high < low, len_row_ref[...], 0).astype(F32), 1, keepdims=True)
    start_row = jnp.sum(jnp.where(low < high, len_col_ref[...], 0).astype(F32), 0, keepdims=True)
    finish_col = start_col + len_col_ref[...].astype(F32)
    finish_row = start_row + len_row_ref[...].astype(F32)
    reached = jnp.where((parent_ref[...] == high) | (low == high), 1.0, 0.0)
    for sweep in range(max(1, (segs - 1).bit_length())):
        low_bits = reached.astype(BF16)
        reached = jnp.minimum(dot(low_bits, low_bits), 1.0)
    me = me_ref[0]
    query_pos = (me * rows + iota((rows, 1), 0)).astype(F32)
    member = jnp.where((query_pos >= start_row) & (query_pos < finish_row), 1.0, 0.0)
    query_reach = dot(member.astype(BF16), reached.astype(BF16)).astype(BF16)
    x, y, core = me // 4, (me // 2) % 2, me % 2
    blocks = bias_ref.shape[1] // rows
    for n in range(blocks):
        half, inner = n // (blocks // 2), n % (blocks // 2)
        other = ((x + 4 - inner // 2) % 4) * 4 + (y + inner) % 2 * 2 + (core + half) % 2
        key_pos = (other * rows + iota((1, rows), 1)).astype(F32)
        holds = jnp.where((key_pos >= start_col) & (key_pos < finish_col), 1.0, 0.0)
        linked = dot(query_reach, holds.astype(BF16))
        visible = (linked > 0.5) & (key_pos <= query_pos)
        bias_ref[:, n * rows : (n + 1) * rows] = jnp.where(visible, 0.0, HIDDEN)
    dispatch(cot_ref[...], slot_keys(ids_t_ref[...], groups), send_ref)


def attend_body(
    groups,
    q_ref,
    own_ref,
    pair_ref,
    near_ref,
    far_ref,
    last_ref,
    core_ref,
    bias_ref,
    residual_ref,
    gain_ref,
    ids_t_ref,
    stream_ref,
    send_ref,
    kv_ref,
):
    first = 0
    for piece in (own_ref, pair_ref, near_ref, far_ref, last_ref, core_ref):
        kv_ref[first : first + piece.shape[0], :] = piece[...]
        first += piece.shape[0]
    kv_heads = kv_ref.shape[1] // (2 * HEAD_DIM)
    per_kv = q_ref.shape[1] // HEAD_DIM // kv_heads
    factor = HEAD_DIM**-0.5 * math.log2(math.e)
    for g in range(kv_heads):

        def head(i, carry):
            columns = pl.ds(pl.multiple_of((g * per_kv + i) * HEAD_DIM, HEAD_DIM), HEAD_DIM)
            keys = kv_ref[:, g * HEAD_DIM : (g + 1) * HEAD_DIM]
            vals = kv_ref[:, (kv_heads + g) * HEAD_DIM : (kv_heads + g + 1) * HEAD_DIM]
            scores = dot_nt(q_ref[:, columns], keys) + bias_ref[...]
            top = jnp.max(scores, -1, keepdims=True)
            probs = jnp.exp2((scores - top) * factor)
            denom = jnp.sum(probs, -1, keepdims=True)
            attended = (dot(probs.astype(BF16), vals) / denom).astype(BF16)
            stream_ref[:, columns] = residual_ref[:, columns].astype(F32) + attended.astype(F32)
            return carry

        lax.fori_loop(0, per_kv, head, 0)
    stream = stream_ref[...]
    scale_back = lax.rsqrt(jnp.mean(stream * stream, -1, keepdims=True) + 1e-06)
    normed = (stream * scale_back * gain_ref[...]).astype(BF16)
    dispatch(normed, slot_keys(ids_t_ref[...], groups), send_ref)


def expert_body(rows_ref, grads_ref, w_ref, out_ref, x_ref, g_ref):
    width = w_ref.shape[0]
    hidden = w_ref.shape[1] // 3
    main = rows_ref.shape[0]
    part = width // 4
    tails = main // 4

    def unpack(source, target):
        target[:main, :] = source[:, :width]
        tail = source[:, width:]
        at = iota((tails, main), 1) - 4 * iota((tails, main), 0)
        for k in range(4):
            pick = jnp.where(at == k, 1.0, 0.0).astype(BF16)
            target[main:, k * part : (k + 1) * part] = dot(pick, tail).astype(BF16)

    def pack(rows, first):
        out_ref[:, first : first + width] = rows[:main, :]
        at = iota((main, tails), 0) - 4 * iota((main, tails), 1)
        tail = jnp.zeros((main, part), F32)
        for k in range(4):
            pick = jnp.where(at == k, 1.0, 0.0).astype(BF16)
            tail = tail + dot(pick, rows[main:, k * part : (k + 1) * part])
        out_ref[:, first + width : first + width + part] = tail.astype(BF16)

    unpack(rows_ref, x_ref)
    unpack(grads_ref, g_ref)
    both = dot(x_ref[...], w_ref[:, : 2 * hidden])
    gate, up = both[:, :hidden], both[:, hidden:]
    sig = jax.nn.sigmoid(gate)
    silu = gate * sig
    activated = (silu * up).astype(BF16)
    pack(dot_nt(activated, w_ref[:, 2 * hidden :]).astype(BF16), 0)
    back = dot(g_ref[...], w_ref[:, 2 * hidden :])
    d_gate = (back * up * sig * (1.0 + gate * (1.0 - sig))).astype(BF16)
    d_up = (back * silu).astype(BF16)
    grad = dot_nt(d_gate, w_ref[:, :hidden]) + dot_nt(d_up, w_ref[:, hidden : 2 * hidden])
    pack(grad.astype(BF16), width + part)


def combine_body(groups, back_ref, stream_ref, cot_ref, gain_ref, ids_ref, weight_ref, mixed_ref, grad_ref, moe_ref, sum_ref):
    tokens, width = stream_ref.shape
    part = width // 4
    rows = groups * BLOCK
    group = iota((tokens, groups), 1)
    named = jnp.zeros((tokens, groups), F32)
    factor = jnp.zeros((tokens, groups), F32)
    for route in range(ids_ref.shape[1]):
        hit = ids_ref[:, route : route + 1] == group
        named = named + jnp.where(hit, 1.0, 0.0)
        factor = factor + jnp.where(hit, weight_ref[:, route : route + 1], 0.0)
    before = jnp.where(iota((tokens, tokens), 1) < iota((tokens, tokens), 0), 1.0, 0.0)
    rank = dot(before.astype(BF16), named.astype(BF16))
    key = jnp.where(named > 0.5, rank, NO_SLOT).astype(BF16)
    spread = jnp.where(iota((groups, rows), 1) // BLOCK == iota((groups, rows), 0), 1.0, 0.0).astype(BF16)
    keys = dot(key, spread)
    coarse = factor.astype(BF16)
    fine = (factor - coarse.astype(F32)).astype(BF16)
    coarse, fine = dot(coarse, spread), dot(fine, spread)
    place = iota((tokens, rows), 1)
    on_time = keys == (place % BLOCK).astype(F32)
    late = keys == (BLOCK + (place % BLOCK) // 4).astype(F32)

    def weighted(mask, rows_back):
        a = jnp.where(mask, coarse, 0.0).astype(BF16)
        b = jnp.where(mask, fine, 0.0).astype(BF16)
        return dot(a, rows_back) + dot(b, rows_back)

    for first, target in ((0, moe_ref), (width + part, sum_ref)):
        target[...] = weighted(on_time, back_ref[:, first : first + width])
        tail = back_ref[:, first + width : first + width + part]
        for k in range(4):
            target[:, k * part : (k + 1) * part] += weighted(late & (place % 4 == k), tail)
    stream = stream_ref[...]
    mixed_ref[...] = (stream + moe_ref[...]).astype(BF16)
    scale_back = lax.rsqrt(jnp.mean(stream * stream, -1, keepdims=True) + 1e-06)
    gain_grad = gain_ref[...] * sum_ref[...]
    inner = jnp.mean(stream * gain_grad, -1, keepdims=True)
    grad_ref[...] = cot_ref[...].astype(F32) + scale_back * gain_grad - stream * (scale_back**3 * inner)


def on_device(
    queries,
    key_rows,
    values,
    residual,
    seg_lengths,
    seg_parent,
    ln_gain,
    w_gate,
    w_up,
    w_down,
    expert_ids,
    gate_weights,
    cotangent,
):
    groups = lax.axis_size("exp")
    members = lax.axis_size("ctx")
    tokens, width = residual.shape[1], residual.shape[2]
    kv_width = key_rows.shape[2] + values.shape[2]
    hidden = w_gate.shape[2]
    slab = members * tokens
    rows = groups * BLOCK
    packed = width + width // 4
    shape = jax.ShapeDtypeStruct
    me = lax.axis_index("ctx").astype(jnp.int32).reshape(1)
    ids_t = expert_ids[0].T
    gain = ln_gain.reshape(1, width)

    kv, w_own = call(pack_body, (shape((tokens, kv_width), BF16), shape((tokens, 3 * hidden), BF16)))(
        key_rows[0], values[0], w_gate[0], w_up[0], w_down[0]
    )

    def send(rows_out, target):
        return lax.ppermute(rows_out, "ctx", [(i, target(i)) for i in range(members)])

    def along_x(i, step):
        return (i // 4 + step) % 4 * 4 + i % 4

    pair = send(kv, lambda i: i ^ 2)
    both = jnp.concatenate([kv, pair], 0)
    near, far, last = (send(both, functools.partial(along_x, step=step)) for step in (1, 2, 3))
    mine = jnp.concatenate([both, near, far, last], 0)
    other_core = send(mine, lambda i: i ^ 1)

    weights = lax.all_gather(w_own, "ctx", axis=0, tiled=True)

    in_smem = pl.BlockSpec(memory_space=pltpu.SMEM)
    in_vmem = pl.BlockSpec(memory_space=pltpu.VMEM)
    bias, send_grad = pl.pallas_call(
        functools.partial(prepare_body, groups),
        out_shape=(shape((tokens, slab), F32), shape((rows, packed), BF16)),
        in_specs=[in_smem] + [in_vmem] * 5,
        out_specs=(in_vmem, in_vmem),
        compiler_params=pltpu.CompilerParams(vmem_limit_bytes=48 << 20),
    )(me, cotangent[0], ids_t, seg_lengths, seg_lengths.reshape(-1, 1), seg_parent.reshape(-1, 1))

    def exchange(sent):
        return lax.all_to_all(
            sent.reshape(groups, BLOCK, sent.shape[1]), "exp", split_axis=0, concat_axis=0, tiled=True
        ).reshape(sent.shape)

    arrived_grad = exchange(send_grad)
    stream, send_input = call(
        functools.partial(attend_body, groups),
        (shape((tokens, width), F32), shape((rows, packed), BF16)),
        [pltpu.VMEM((slab, kv_width), BF16)],
        flops=4 * tokens * slab * width,
        moved=8 << 20,
    )(queries[0], kv, pair, near, far, last, other_core, bias, residual[0], gain, ids_t)
    arrived_in = exchange(send_input)
    returned = call(
        expert_body,
        shape((rows, 2 * packed), BF16),
        [pltpu.VMEM((groups * CAP, width), BF16)] * 2,
        flops=12 * groups * CAP * width * hidden,
        moved=10 << 20,
    )(arrived_in, arrived_grad, weights)
    back = exchange(returned)
    mixed_out, stream_grad = call(
        functools.partial(combine_body, groups),
        (shape((tokens, width), BF16), shape((tokens, width), F32)),
        [pltpu.VMEM((tokens, width), F32)] * 2,
    )(back, stream, cotangent[0], gain, expert_ids[0], gate_weights[0])
    return (mixed_out[None], stream_grad[None])


def solution(mesh):
    placed = (
        P("exp", "ctx", None),
        P("exp", "ctx", None),
        P("exp", "ctx", None),
        P("exp", "ctx", None),
        P("exp", None),
        P("exp", None),
        P(),
        P("exp", "ctx", None),
        P("exp", "ctx", None),
        P("exp", None, "ctx"),
        P("exp", "ctx", None),
        P("exp", "ctx", None),
        P("exp", "ctx", None),
    )
    return jax.shard_map(
        on_device,
        mesh=mesh,
        in_specs=placed,
        out_specs=(P("exp", "ctx", None), P("exp", "ctx", None)),
        check_vma=False,
    )
```

time: 506 us -> 254 us (0.50)
  the two profiles are of different devices: /device:TPU:56 before, /device:TPU:98 now
where the time goes in v1:
time: 254 us; the launch traced here: 253 us
  waiting for transfers between devices  120 us (47%)
  blocking collectives  43.5 us (17%)
  starting transfers between devices  33.2 us (13%)
  Pallas kernels  29.5 us (12%)
  between operations  14.2 us (6%)
  local copies, waits for them, and re-layouts  12.2 us (5%)
    all_to_all x2, waiting for transfers between devices, exchange(): lax.all_to_all(sent.reshape(groups, BLOCK, sent.shape[1]), 'exp', split_a...  73.2 us
    ppermute x5, waiting for transfers between devices, send(): lax.ppermute(rows_out, 'ctx', [(i, target(i)) for i in range(members)])  46.9 us
    all_to_all x1, blocking collectives, exchange(): lax.all_to_all(sent.reshape(groups, BLOCK, sent.shape[1]), 'exp', split_a...  43.5 us
    ppermute x5, starting transfers between devices, send(): lax.ppermute(rows_out, 'ctx', [(i, target(i)) for i in range(members)])  17.2 us
    all_to_all x2, starting transfers between devices, exchange(): lax.all_to_all(sent.reshape(groups, BLOCK, sent.shape[1]), 'exp', split_a...  15.9 us
    pallas_call x1, Pallas kernels, on_device(): call(functools.partial(attend_body, groups), (shape((tokens, width), F32)...  14.7 us
    unnamed x40, local copies, waits for them, and re-layouts  10.7 us
    pallas_call x1, Pallas kernels, on_device(): call(expert_body, shape((rows, 2 * packed), BF16), [pltpu.VMEM((groups *...  7.97 us
  transfers between devices with their start and end apart: 8, of which 6 were waited for; matrix products, arithmetic and copies ran while one was open for 1% of the time, Pallas kernels for 7%

profile of v1, /device:TPU:98, one launch (start us, length us, event | category | flops | bytes accessed | tf_op | source)
XLA Modules:
  0.0 252.7 jit_solution(16221425731249163270)
XLA Ops:
  7.2 0.0 all-gather.2.cloned.1.call-start
  7.2 0.0 copy-start.5
  7.2 0.9 copy-done.5
  8.1 0.0 copy-start.6
  8.1 0.9 copy-done.6
  9.0 0.0 copy-start.7
  9.0 0.9 copy-done.7
  9.9 0.0 copy-start.8
  9.9 0.8 copy-done.8
  10.7 0.0 copy-start.9
  10.7 0.8 copy-done.9
  11.6 0.8 shard_map.140
  12.4 0.0 all-gather.2.cloned.1.call-update
  12.4 0.7 copy.17.len_col_ref
  13.1 0.7 copy.18.parent_ref
  13.9 0.0 copy-start.1
  13.9 1.0 copy-done.1
  14.9 0.0 copy-start.10
  14.9 0.7 copy-done.10
  15.6 0.0 copy-start.13
  15.6 0.7 copy-done.13
  16.3 3.0 %shard_map.141 = (f32[128,2048]{1,0:T(8,128)S(1)}, bf16[256,2560]{1,0:T(8,128)(2,1)}) custom-call(s32[1]{0:T(128)} %bitcast.6.me_ref, bf16[128,2048]{1,0:T(8,128)(2,1)S(1)} %bitcast.26, s32[8,128]{1,0:T(8,128)S(1)} %bitcast.37, s32[1,32]{1,0:T(1,128)S(1)} %copy-done.13, s32[32,1]{1,0:T(8,128)S(1)} %copy.17.len_col_ref, s32[32,1]{1,0:T(8,128)S(1)} %copy.18.parent_ref), custom_call_target="tpu_custom_call" | custom-call | tf_op jit(solution)/shard_map/pallas_call | solution.py:282
  19.3 10.5 %all-to-all-start.1 = ((bf16[32,8,2560]{2,1,0:T(8,128)(2,1)}), bf16[32,8,2560]{2,1,0:T(8,128)(2,1)S(1)}, u32[]{:S(2)}, u32[]{:S(2)}) async-start(bf16[32,8,2560]{2,1,0:T(8,128)(2,1)} %bitcast.17), calls=%async_computation.1 | async-start | bytes 2621440 | tf_op jit(solution)/shard_map/all_to_all | solution.py:291
  29.7 0.0 copy-start.11
  29.8 0.0 copy-start.12
  29.8 0.0 copy-start.14
  29.8 0.0 copy-start.15
  29.8 4.8 %collective-permute-start = (bf16[128,512]{1,0:T(8,128)(2,1)S(1)}, bf16[128,512]{1,0:T(8,128)(2,1)S(1)}, u32[]{:S(2)}, u32[]{:S(2)}) collective-permute-start(bf16[128,512]{1,0:T(8,128)(2,1)S(1)} %get-tuple-element.10.own_ref), channel_id=1, source_target_pairs={{0,64},{32,96},{64,0},{96,32},{128,192},{160,224},{192,128},{224,1... | collective-permute-start | bytes 393224 | tf_op jit(solution)/shard_map/ppermute | solution.py:267
  34.7 31.1 %collective-permute-done.pair_ref = bf16[128,512]{1,0:T(8,128)(2,1)S(1)} collective-permute-done((bf16[128,512]{1,0:T(8,128)(2,1)S(1)}, bf16[128,512]{1,0:T(8,128)(2,1)S(1)}, u32[]{:S(2)}, u32[]{:S(2)}) %collective-permute-start) | collective-permute-done | bytes 131104 | tf_op jit(solution)/shard_map/ppermute | solution.py:267
  65.8 3.4 %collective-permute-start.1 = (bf16[256,512]{1,0:T(8,128)(2,1)S(1)}, bf16[256,512]{1,0:T(8,128)(2,1)S(1)}, u32[]{:S(2)}, u32[]{:S(2)}) collective-permute-start(bf16[256,512]{1,0:T(8,128)(2,1)S(1)} %get-tuple-element.19), channel_id=1, source_target_pairs={{0,128},{32,160},{64,192},{96,224},{128,256},{160,288},{192,320},{... | collective-permute-start | bytes 786440 | tf_op jit(solution)/shard_map/ppermute | solution.py:267
  69.2 3.0 %collective-permute-start.2 = (bf16[256,512]{1,0:T(8,128)(2,1)S(1)}, bf16[256,512]{1,0:T(8,128)(2,1)S(1)}, u32[]{:S(2)}, u32[]{:S(2)}) collective-permute-start(bf16[256,512]{1,0:T(8,128)(2,1)S(1)} %get-tuple-element.19), channel_id=1, source_target_pairs={{0,256},{32,288},{64,320},{96,352},{128,384},{160,416},{192,448},{... | collective-permute-start | bytes 786440 | tf_op jit(solution)/shard_map/ppermute | solution.py:267
  72.3 4.0 %collective-permute-start.3 = (bf16[256,512]{1,0:T(8,128)(2,1)S(1)}, bf16[256,512]{1,0:T(8,128)(2,1)S(1)}, u32[]{:S(2)}, u32[]{:S(2)}) collective-permute-start(bf16[256,512]{1,0:T(8,128)(2,1)S(1)} %get-tuple-element.19), channel_id=1, source_target_pairs={{0,384},{32,416},{64,448},{96,480},{128,0},{160,32},{192,64},{224,... | collective-permute-start | bytes 786440 | tf_op jit(solution)/shard_map/ppermute | solution.py:267
  76.3 2.4 collective-permute-done.1.near_ref
  78.8 3.8 %collective-permute-done.2.far_ref = bf16[256,512]{1,0:T(8,128)(2,1)S(1)} collective-permute-done((bf16[256,512]{1,0:T(8,128)(2,1)S(1)}, bf16[256,512]{1,0:T(8,128)(2,1)S(1)}, u32[]{:S(2)}, u32[]{:S(2)}) %collective-permute-start.2) | collective-permute-done | bytes 262176 | tf_op jit(solution)/shard_map/ppermute | solution.py:267
  82.6 6.9 %collective-permute-done.3.last_ref = bf16[256,512]{1,0:T(8,128)(2,1)S(1)} collective-permute-done((bf16[256,512]{1,0:T(8,128)(2,1)S(1)}, bf16[256,512]{1,0:T(8,128)(2,1)S(1)}, u32[]{:S(2)}, u32[]{:S(2)}) %collective-permute-start.3) | collective-permute-done | bytes 262176 | tf_op jit(solution)/shard_map/ppermute | solution.py:267
  89.5 1.9 collective-permute-start.4
  91.4 2.6 %collective-permute-done.4.core_ref = bf16[1024,512]{1,0:T(8,128)(2,1)S(1)} collective-permute-done((bf16[1024,512]{1,0:T(8,128)(2,1)S(1)}, bf16[1024,512]{1,0:T(8,128)(2,1)S(1)}, u32[]{:S(2)}, u32[]{:S(2)}) %collective-permute-start.4) | collective-permute-done | bytes 1048608 | tf_op jit(solution)/shard_map/ppermute | solution.py:267
  94.1 0.0 copy-done.11
  94.1 0.0 copy-done.12
  94.1 0.0 copy-done.14
  94.1 0.0 copy-done.15
  94.1 14.7 %shard_map.142 = (f32[128,2048]{1,0:T(8,128)S(1)}, bf16[256,2560]{1,0:T(8,128)(2,1)}) custom-call(bf16[128,2048]{1,0:T(8,128)(2,1)S(1)} %bitcast.42, bf16[128,512]{1,0:T(8,128)(2,1)S(1)} %get-tuple-element.10.own_ref, bf16[128,512]{1,0:T(8,128)(2,1)S(1)} %collective-permute-done.pair_ref, bf16[256,512]{1,0:T(8,128)(2,1)S(1)} %collective-permute-done.1.near_ref, ...), custom_call_target="tpu_custom_call" | custom-call | flops 2147483648 | bytes 8388608 | tf_op jit(solution)/shard_map/pallas_call | solution.py:296
  108.8 0.0 copy-start.3
  108.8 1.0 copy-done.3
  109.8 0.0 all-to-all-done.1
  109.8 43.5 %all_to_all.15 = bf16[32,8,2560]{2,1,0:T(8,128)(2,1)S(1)} all-to-all(bf16[32,8,2560]{2,1,0:T(8,128)(2,1)} %bitcast.44), channel_id=1, replica_groups=mesh['ctx'=16,'exp'=32] {'exp'}, dimensions={0} | all-to-all | bytes 2621440 | tf_op jit(solution)/shard_map/all_to_all | solution.py:291
  153.3 0.0 all-gather.2.cloned.1.call-done.w_ref
  153.3 8.0 %shard_map.143 = bf16[256,5120]{1,0:T(8,128)(2,1)S(1)} custom-call(bf16[256,2560]{1,0:T(8,128)(2,1)S(1)} %bitcast.29, bf16[256,2560]{1,0:T(8,128)(2,1)S(1)} %bitcast.28, bf16[2048,1152]{1,0:T(8,128)(2,1)} %all-gather.2.cloned.1.call-done.w_ref), custom_call_target="tpu_custom_call" | custom-call | flops 3019898880 | bytes 10485760 | tf_op jit(solution)/shard_map/pallas_call | solution.py:304
  161.3 0.0 copy-start
  161.3 1.5 copy-done
  162.8 0.0 copy-start.16
  162.8 0.0 copy-start.2
  162.8 5.4 %all-to-all-start.2 = ((bf16[32,8,5120]{2,1,0:T(8,128)(2,1)}), bf16[32,8,5120]{2,1,0:T(8,128)(2,1)S(1)}, u32[]{:S(2)}, u32[]{:S(2)}) async-start(bf16[32,8,5120]{2,1,0:T(8,128)(2,1)} %bitcast.25), calls=%async_computation.2 | async-start | bytes 5242880 | tf_op jit(solution)/shard_map/all_to_all | solution.py:291
  168.2 0.1 copy.15
  168.3 0.0 copy-done.16
  168.3 0.1 copy.20
  168.4 73.2 %all-to-all-done.2 = bf16[32,8,5120]{2,1,0:T(8,128)(2,1)S(1)} async-done(((bf16[32,8,5120]{2,1,0:T(8,128)(2,1)}), bf16[32,8,5120]{2,1,0:T(8,128)(2,1)S(1)}, u32[]{:S(2)}, u32[]{:S(2)}) %all-to-all-start.2) | async-done | bytes 2621472 | tf_op jit(solution)/shard_map/all_to_all | solution.py:291
  241.6 0.0 copy-done.2
  241.6 0.0 copy-start.4
  241.6 1.2 copy-done.4
  242.8 3.0 %shard_map.144 = (bf16[128,2048]{1,0:T(8,128)(2,1)}, f32[128,2048]{1,0:T(8,128)}) custom-call(bf16[256,5120]{1,0:T(8,128)(2,1)S(1)} %bitcast.24, f32[128,2048]{1,0:T(8,128)S(1)} %copy-done.4, bf16[128,2048]{1,0:T(8,128)(2,1)S(1)} %bitcast.27, f32[1,2048]{1,0:T(1,128)S(1)} %bitcast.40, s32[128,8]{1,0:T(8,128)S(1)} %bitcast.30, f32[128,8]{1,0:T(8,128)S(1)} %bitcast.31), custom_call_target="tpu_custom_call" | custom-call | tf_op jit(solution)/shard_map/pallas_call | solution.py:312
  (5 shorter events, 0.1 us)
Async XLA Ops:
  7.2 146.1 %all-gather.2.cloned.1.call-start = ((), (), s32[]{:S(2)}) async-start(), calls=%async_computation.3 | async-start | bytes 5013504 | tf_op jit(solution)/shard_map/all_gather | solution.py:278
  7.2 0.9 copy-start.5
  8.1 0.9 copy-start.6
  9.0 0.9 copy-start.7
  9.9 0.8 copy-start.8
  10.7 0.8 copy-start.9
  13.9 1.0 copy-start.1
  14.9 0.7 copy-start.10
  15.6 0.7 copy-start.13
  19.3 90.5 %all-to-all-start.1 = ((bf16[32,8,2560]{2,1,0:T(8,128)(2,1)}), bf16[32,8,2560]{2,1,0:T(8,128)(2,1)S(1)}, u32[]{:S(2)}, u32[]{:S(2)}) async-start(bf16[32,8,2560]{2,1,0:T(8,128)(2,1)} %bitcast.17), calls=%async_computation.1 | async-start | bytes 2621440 | tf_op jit(solution)/shard_map/all_to_all | solution.py:291
  29.7 64.3 %copy-start.11 = (s32[1,128,8]{1,2,0:T(8,128)S(1)}, s32[1,128,8]{1,2,0:T(8,128)}, u32[]{:S(2)}) copy-start(s32[1,128,8]{1,2,0:T(8,128)} %param.23) | copy-start | bytes 12292
  29.8 64.3 %copy-start.12 = (f32[2048]{0:T(1024)S(1)}, f32[2048]{0:T(1024)}, u32[]{:S(2)}) copy-start(f32[2048]{0:T(1024)} %param.19) | copy-start | bytes 24580
  29.8 64.3 %copy-start.14 = (bf16[1,128,2048]{2,1,0:T(8,128)(2,1)S(1)}, bf16[1,128,2048]{2,1,0:T(8,128)(2,1)}, u32[]{:S(2)}) copy-start(bf16[1,128,2048]{2,1,0:T(8,128)(2,1)} %param.13) | copy-start | bytes 1572868
  29.8 64.3 %copy-start.15 = (bf16[1,128,2048]{2,1,0:T(8,128)(2,1)S(1)}, bf16[1,128,2048]{2,1,0:T(8,128)(2,1)}, u32[]{:S(2)}) copy-start(bf16[1,128,2048]{2,1,0:T(8,128)(2,1)} %param.16) | copy-start | bytes 1572868
  29.8 36.0 %collective-permute-start = (bf16[128,512]{1,0:T(8,128)(2,1)S(1)}, bf16[128,512]{1,0:T(8,128)(2,1)S(1)}, u32[]{:S(2)}, u32[]{:S(2)}) collective-permute-start(bf16[128,512]{1,0:T(8,128)(2,1)S(1)} %get-tuple-element.10.own_ref), channel_id=1, source_target_pairs={{0,64},{32,96},{64,0},{96,32},{128,192},{160,224},{192,128},{224,1... | collective-permute-start | bytes 393224 | tf_op jit(solution)/shard_map/ppermute | solution.py:267
  65.8 12.9 %collective-permute-start.1 = (bf16[256,512]{1,0:T(8,128)(2,1)S(1)}, bf16[256,512]{1,0:T(8,128)(2,1)S(1)}, u32[]{:S(2)}, u32[]{:S(2)}) collective-permute-start(bf16[256,512]{1,0:T(8,128)(2,1)S(1)} %get-tuple-element.19), channel_id=1, source_target_pairs={{0,128},{32,160},{64,192},{96,224},{128,256},{160,288},{192,320},{... | collective-permute-start | bytes 786440 | tf_op jit(solution)/shard_map/ppermute | solution.py:267
  69.2 13.3 %collective-permute-start.2 = (bf16[256,512]{1,0:T(8,128)(2,1)S(1)}, bf16[256,512]{1,0:T(8,128)(2,1)S(1)}, u32[]{:S(2)}, u32[]{:S(2)}) collective-permute-start(bf16[256,512]{1,0:T(8,128)(2,1)S(1)} %get-tuple-element.19), channel_id=1, source_target_pairs={{0,256},{32,288},{64,320},{96,352},{128,384},{160,416},{192,448},{... | collective-permute-start | bytes 786440 | tf_op jit(solution)/shard_map/ppermute | solution.py:267
  72.3 17.2 %collective-permute-start.3 = (bf16[256,512]{1,0:T(8,128)(2,1)S(1)}, bf16[256,512]{1,0:T(8,128)(2,1)S(1)}, u32[]{:S(2)}, u32[]{:S(2)}) collective-permute-start(bf16[256,512]{1,0:T(8,128)(2,1)S(1)} %get-tuple-element.19), channel_id=1, source_target_pairs={{0,384},{32,416},{64,448},{96,480},{128,0},{160,32},{192,64},{224,... | collective-permute-start | bytes 786440 | tf_op jit(solution)/shard_map/ppermute | solution.py:267
  89.5 4.6 %collective-permute-start.4 = (bf16[1024,512]{1,0:T(8,128)(2,1)S(1)}, bf16[1024,512]{1,0:T(8,128)(2,1)S(1)}, u32[]{:S(2)}, u32[]{:S(2)}) collective-permute-start(bf16[1024,512]{1,0:T(8,128)(2,1)S(1)} %constant_dynamic-update-slice_fusion.2), channel_id=1, source_target_pairs={{0,32},{32,0},{64,96},{96,64},{128,160},{160,128},{192,224},{224,1... | collective-permute-start | bytes 3145736 | tf_op jit(solution)/shard_map/ppermute | solution.py:267
  108.8 1.0 copy-start.3
  161.3 1.5 copy-start
  162.8 5.5 %copy-start.16 = (f32[1,128,8]{1,2,0:T(8,128)S(1)}, f32[1,128,8]{1,2,0:T(8,128)}, u32[]{:S(2)}) copy-start(f32[1,128,8]{1,2,0:T(8,128)} %param.24) | copy-start | bytes 12292
  162.8 78.8 %copy-start.2 = (bf16[1,128,2048]{2,1,0:T(8,128)(2,1)S(1)}, bf16[1,128,2048]{2,1,0:T(8,128)(2,1)}, u32[]{:S(2)}) copy-start(bf16[1,128,2048]{2,1,0:T(8,128)(2,1)} %param.25) | copy-start | bytes 1572868
  162.8 78.8 %all-to-all-start.2 = ((bf16[32,8,5120]{2,1,0:T(8,128)(2,1)}), bf16[32,8,5120]{2,1,0:T(8,128)(2,1)S(1)}, u32[]{:S(2)}, u32[]{:S(2)}) async-start(bf16[32,8,5120]{2,1,0:T(8,128)(2,1)} %bitcast.25), calls=%async_computation.2 | async-start | bytes 5242880 | tf_op jit(solution)/shard_map/all_to_all | solution.py:291
  241.6 1.2 copy-start.4
Sparse Core Ops, SparseCore 0:
  12.5 81.7 all-gather.1

commit v2 on v1

v2 whole, which is shorter than its diff:
```python
import functools
import math

import jax
import jax.numpy as jnp
from jax import lax
from jax.experimental import pallas as pl
from jax.experimental.pallas import tpu as pltpu
from jax.sharding import PartitionSpec as P

HEAD_DIM = 128
TOPK = 8
CAP = 10
BLOCK = 8
NO_SLOT = 512.0
TOGETHER = 4
ROOMY = 28 << 20
ALONE = 60 << 20
HIDDEN = -1e30
F32 = jnp.float32
BF16 = jnp.bfloat16
NT = (((1,), (1,)), ((), ()))


def iota(shape, dim):
    return lax.broadcasted_iota(jnp.int32, shape, dim)


def dot(a, b):
    return jnp.dot(a, b, preferred_element_type=F32)


def dot_nt(a, b):
    return lax.dot_general(a, b, NT, preferred_element_type=F32)


def call(body, outs, scratch=(), in_specs=None, out_specs=None, flops=0, moved=0, vmem=ALONE):
    specs = {} if in_specs is None else {"in_specs": in_specs, "out_specs": out_specs}
    return pl.pallas_call(
        body,
        out_shape=outs,
        **specs,
        scratch_shapes=list(scratch),
        compiler_params=pltpu.CompilerParams(vmem_limit_bytes=vmem),
        cost_estimate=pl.CostEstimate(flops=flops, bytes_accessed=moved, transcendentals=0),
    )


def slot_keys(ids_t, groups):
    tokens = ids_t.shape[1]
    group = iota((groups, tokens), 0)
    named = jnp.zeros((groups, tokens), F32)
    for route in range(ids_t.shape[0]):
        named = named + jnp.where(ids_t[route : route + 1, :] == group, 1.0, 0.0)
    before = (iota((tokens, tokens), 0) < iota((tokens, tokens), 1)).astype(F32)
    rank = dot(named.astype(BF16), before.astype(BF16))
    key = jnp.where(named > 0.5, rank, NO_SLOT).astype(BF16)
    rows = groups * BLOCK
    spread = (iota((rows, groups), 0) // BLOCK == iota((rows, groups), 1)).astype(F32)
    return dot(spread.astype(BF16), key)


def dispatch(rows, keys, out_ref):
    place = iota(keys.shape, 0)
    width = rows.shape[1]
    part = width // 4
    pick = jnp.where(keys == (place % BLOCK).astype(F32), 1.0, 0.0).astype(BF16)
    out_ref[:, :width] = dot(pick, rows).astype(BF16)
    late = keys == (BLOCK + (place % BLOCK) // 4).astype(F32)
    tail = jnp.zeros((keys.shape[0], part), F32)
    for k in range(4):
        pick = jnp.where(late & (place % 4 == k), 1.0, 0.0).astype(BF16)
        tail = tail + dot(pick, rows[:, k * part : (k + 1) * part])
    out_ref[:, width:] = tail.astype(BF16)


def copy_all(copies):
    for one in copies:
        one.start()
    for one in copies:
        one.wait()


def pack_kv_body(key_hbm, value_hbm, kv_hbm, kv_ref, sems):
    half = key_hbm.shape[1]
    copy_all(
        [
            pltpu.make_async_copy(key_hbm, kv_ref.at[:, pl.ds(0, half)], sems.at[0]),
            pltpu.make_async_copy(value_hbm, kv_ref.at[:, pl.ds(half, half)], sems.at[1]),
        ]
    )
    copy_all([pltpu.make_async_copy(kv_ref, kv_hbm, sems.at[2])])


def pack_w_body(gate_hbm, up_hbm, down_hbm, w_hbm, down_ref, w_ref, sems):
    hidden = gate_hbm.shape[1]
    copies = [
        pltpu.make_async_copy(down_hbm, down_ref, sems.at[0]),
        pltpu.make_async_copy(gate_hbm, w_ref.at[:, pl.ds(0, hidden)], sems.at[1]),
        pltpu.make_async_copy(up_hbm, w_ref.at[:, pl.ds(hidden, hidden)], sems.at[2]),
    ]
    copy_all(copies)
    w_ref[:, 2 * hidden :] = down_ref[...].T
    copy_all([pltpu.make_async_copy(w_ref, w_hbm, sems.at[3])])


def place_of(me, n):
    x, y, core = me // 4, (me // 2) % 2, me % 2
    return (x + 4 - n % 8 // 2) % 4 * 4 + (y + n) % 2 * 2 + (core + n // 8) % 2


def stack_body(count, *refs):
    out_ref, sems = refs[-2:]
    first, copies = 0, []
    for n, piece in enumerate(refs[:count]):
        copies.append(pltpu.make_async_copy(piece, out_ref.at[pl.ds(first, piece.shape[0])], sems.at[n]))
        first += piece.shape[0]
    copy_all(copies)


def tie_body(array_ref, after_ref, out_ref):
    del array_ref, after_ref, out_ref


def scatter_body(groups, rows_hbm, ids_hbm, send_hbm, rows_ref, ids_ref, send_ref, sems):
    get_ids = pltpu.make_async_copy(ids_hbm, ids_ref, sems.at[0])
    get_rows = pltpu.make_async_copy(rows_hbm, rows_ref, sems.at[1])
    get_ids.start()
    get_rows.start()
    get_ids.wait()
    keys = slot_keys(ids_ref[...], groups)
    get_rows.wait()
    dispatch(rows_ref[...], keys, send_ref)
    copy_all([pltpu.make_async_copy(send_ref, send_hbm, sems.at[2])])


def bias_body(me_ref, len_hbm, parent_hbm, bias_hbm, len_ref, parent_ref, bias_ref, sems):
    copy_all(
        [
            pltpu.make_async_copy(len_hbm, len_ref, sems.at[0]),
            pltpu.make_async_copy(parent_hbm, parent_ref, sems.at[1]),
        ]
    )
    segs = len_ref.shape[1]
    rows = bias_ref.shape[0]
    low, high = iota((segs, segs), 0), iota((segs, segs), 1)
    len_row = len_ref[...].astype(F32)
    len_col = jnp.sum(jnp.where(low == high, len_row, 0.0), 1, keepdims=True)
    parent_col = jnp.sum(jnp.where(low == high, parent_ref[...].astype(F32), 0.0), 1, keepdims=True)
    start_col = jnp.sum(jnp.where(high < low, len_row, 0.0), 1, keepdims=True)
    start_row = jnp.sum(jnp.where(low < high, len_col, 0.0), 0, keepdims=True)
    finish_col = start_col + len_col
    finish_row = start_row + len_row
    reached = jnp.where((parent_col == high.astype(F32)) | (low == high), 1.0, 0.0)
    for sweep in range(max(1, (segs - 1).bit_length())):
        low_bits = reached.astype(BF16)
        reached = jnp.minimum(dot(low_bits, low_bits), 1.0)
    me = me_ref[0]
    query_pos = (me * rows + iota((rows, 1), 0)).astype(F32)
    member = jnp.where((query_pos >= start_row) & (query_pos < finish_row), 1.0, 0.0)
    query_reach = dot(member.astype(BF16), reached.astype(BF16)).astype(BF16)
    for n in range(bias_ref.shape[1] // rows):
        key_pos = (place_of(me, n) * rows + iota((1, rows), 1)).astype(F32)
        holds = jnp.where((key_pos >= start_col) & (key_pos < finish_col), 1.0, 0.0)
        linked = dot(query_reach, holds.astype(BF16))
        visible = (linked > 0.5) & (key_pos <= query_pos)
        bias_ref[:, n * rows : (n + 1) * rows] = jnp.where(visible, 0.0, HIDDEN)
    copy_all([pltpu.make_async_copy(bias_ref, bias_hbm, sems.at[2])])


def attend_body(
    groups,
    q_hbm,
    mine_hbm,
    core_hbm,
    residual_hbm,
    bias_hbm,
    gain_hbm,
    ids_hbm,
    stream_hbm,
    send_hbm,
    q_ref,
    kv_ref,
    residual_ref,
    bias_ref,
    gain_ref,
    ids_ref,
    stream_ref,
    send_ref,
    sems,
):
    pieces, first, fetch = (mine_hbm, core_hbm), 0, []
    for n, piece in enumerate(pieces):
        fetch.append(pltpu.make_async_copy(piece, kv_ref.at[pl.ds(first, piece.shape[0])], sems.at[n]))
        first += piece.shape[0]
    fetch += [
        pltpu.make_async_copy(q_hbm, q_ref, sems.at[2]),
        pltpu.make_async_copy(bias_hbm, bias_ref, sems.at[3]),
        pltpu.make_async_copy(residual_hbm, residual_ref, sems.at[6]),
        pltpu.make_async_copy(gain_hbm, gain_ref, sems.at[7]),
        pltpu.make_async_copy(ids_hbm, ids_ref, sems.at[8]),
    ]
    for one in fetch:
        one.start()
    for one in fetch[:4]:
        one.wait()
    kv_heads = kv_ref.shape[1] // (2 * HEAD_DIM)
    per_kv = q_ref.shape[1] // HEAD_DIM // kv_heads
    factor = HEAD_DIM**-0.5 * math.log2(math.e)
    for g in range(kv_heads):
        keys = kv_ref[:, g * HEAD_DIM : (g + 1) * HEAD_DIM]
        vals = kv_ref[:, (kv_heads + g) * HEAD_DIM : (kv_heads + g + 1) * HEAD_DIM]

        def heads(i, carry):
            at = [pl.multiple_of((g * per_kv + i * TOGETHER + j) * HEAD_DIM, HEAD_DIM) for j in range(TOGETHER)]
            scores = [dot_nt(q_ref[:, pl.ds(a, HEAD_DIM)], keys) + bias_ref[...] for a in at]
            for a, score in zip(at, scores):
                top = jnp.max(score, -1, keepdims=True)
                probs = jnp.exp2((score - top) * factor)
                denom = jnp.sum(probs, -1, keepdims=True)
                attended = (dot(probs.astype(BF16), vals) / denom).astype(BF16)
                stream_ref[:, pl.ds(a, HEAD_DIM)] = attended.astype(F32)
            return carry

        lax.fori_loop(0, per_kv // TOGETHER, heads, 0)
    for one in fetch[4:]:
        one.wait()
    stream = residual_ref[...].astype(F32) + stream_ref[...]
    stream_ref[...] = stream
    keep = pltpu.make_async_copy(stream_ref, stream_hbm, sems.at[4])
    keep.start()
    scale_back = lax.rsqrt(jnp.mean(stream * stream, -1, keepdims=True) + 1e-06)
    normed = (stream * scale_back * gain_ref[...]).astype(BF16)
    dispatch(normed, slot_keys(ids_ref[...], groups), send_ref)
    out = pltpu.make_async_copy(send_ref, send_hbm, sems.at[5])
    out.start()
    keep.wait()
    out.wait()


def expert_body(me_ref, rows_hbm, grads_hbm, *refs):
    out_hbm, x_ref, x_tail, g_ref, g_tail, w_ref, out_ref, sems, w_sems, out_sems = refs[-10:]
    width = w_ref.shape[0]
    hidden = w_ref.shape[1] // 3
    main = rows_hbm.shape[0]
    part = width // 4
    tails = main // 4
    blocks = w_sems.shape[1]
    tall = width // blocks
    pieces = [(piece, row) for piece in refs[:-10] for row in range(0, piece.shape[0], tall)]

    def fetch_rows(source, whole, tail, first):
        return [
            pltpu.make_async_copy(source.at[:, pl.ds(0, width)], whole.at[pl.ds(0, main)], sems.at[first]),
            pltpu.make_async_copy(source.at[:, pl.ds(width, part)], tail, sems.at[first + 1]),
        ]

    def fetch_weights(group, first, wide):
        copies = []
        for n in range(blocks):
            piece, row = pieces[n]
            source = piece.at[pl.ds(row, tall), pl.ds(first, wide)]
            rows = pl.ds(pl.multiple_of(place_of(me_ref[0], n) * tall, tall), tall)
            copies.append(pltpu.make_async_copy(source, w_ref.at[rows, pl.ds(first, wide)], w_sems.at[group, n]))
        return copies

    get_rows = fetch_rows(rows_hbm, x_ref, x_tail, 0)
    get_grads = fetch_rows(grads_hbm, g_ref, g_tail, 2)
    get_in = fetch_weights(0, 0, 2 * hidden)
    get_out = fetch_weights(1, 2 * hidden, hidden)
    for one in get_rows + get_in + get_out + get_grads:
        one.start()

    def unpack(tail, target):
        at = iota((tails, main), 1) - 4 * iota((tails, main), 0)
        for k in range(4):
            pick = jnp.where(at == k, 1.0, 0.0).astype(BF16)
            target[main:, k * part : (k + 1) * part] = dot(pick, tail[...]).astype(BF16)

    def pack(rows, index):
        first = index * (width + part)
        out_ref[:, first : first + width] = rows[:main, :]
        at = iota((main, tails), 0) - 4 * iota((main, tails), 1)
        tail = jnp.zeros((main, part), F32)
        for k in range(4):
            pick = jnp.where(at == k, 1.0, 0.0).astype(BF16)
            tail = tail + dot(pick, rows[main:, k * part : (k + 1) * part])
        out_ref[:, first + width : first + width + part] = tail.astype(BF16)
        columns = pl.ds(first, width + part)
        copy = pltpu.make_async_copy(out_ref.at[:, columns], out_hbm.at[:, columns], out_sems.at[index])
        copy.start()
        return copy

    for one in get_rows:
        one.wait()
    unpack(x_tail, x_ref)
    for one in get_in:
        one.wait()
    both = dot(x_ref[...], w_ref[:, : 2 * hidden])
    gate, up = both[:, :hidden], both[:, hidden:]
    sig = jax.nn.sigmoid(gate)
    silu = gate * sig
    activated = (silu * up).astype(BF16)
    for one in get_out:
        one.wait()
    put_out = pack(dot_nt(activated, w_ref[:, 2 * hidden :]).astype(BF16), 0)
    for one in get_grads:
        one.wait()
    unpack(g_tail, g_ref)
    back = dot(g_ref[...], w_ref[:, 2 * hidden :])
    d_gate = (back * up * sig * (1.0 + gate * (1.0 - sig))).astype(BF16)
    d_up = (back * silu).astype(BF16)
    grad = dot_nt(d_gate, w_ref[:, :hidden]) + dot_nt(d_up, w_ref[:, hidden : 2 * hidden])
    put_grad = pack(grad.astype(BF16), 1)
    put_out.wait()
    put_grad.wait()


def factor_body(groups, ids_hbm, weight_hbm, factor_hbm, ids_ref, weight_ref, factor_ref, sems):
    fetch = [
        pltpu.make_async_copy(ids_hbm, ids_ref, sems.at[0]),
        pltpu.make_async_copy(weight_hbm, weight_ref, sems.at[1]),
    ]
    copy_all(fetch)
    tokens = ids_ref.shape[1]
    rows = groups * BLOCK
    group = iota((groups, tokens), 0)
    factor = jnp.zeros((groups, tokens), F32)
    for route in range(ids_ref.shape[0]):
        here = ids_ref[route : route + 1, :] == group
        factor = factor + jnp.where(here, weight_ref[route : route + 1, :], 0.0)
    spread = jnp.where(iota((rows, groups), 0) // BLOCK == iota((rows, groups), 1), 1.0, 0.0).astype(BF16)
    coarse = factor.astype(BF16)
    fine = (factor - coarse.astype(F32)).astype(BF16)
    keys = slot_keys(ids_ref[...], groups).T
    coarse, fine = dot(spread, coarse).T, dot(spread, fine).T
    place = iota((tokens, rows), 1)
    late = keys == (BLOCK + (place % BLOCK) // 4).astype(F32)
    masks = [keys == (place % BLOCK).astype(F32)] + [late & (place % 4 == k) for k in range(4)]
    for n, mask in enumerate(masks):
        factor_ref[:, 2 * n * rows : (2 * n + 1) * rows] = jnp.where(mask, coarse, 0.0).astype(BF16)
        factor_ref[:, (2 * n + 1) * rows : (2 * n + 2) * rows] = jnp.where(mask, fine, 0.0).astype(BF16)
    copy_all([pltpu.make_async_copy(factor_ref, factor_hbm, sems.at[2])])


def combine_body(
    back_hbm, stream_hbm, cot_hbm, gain_hbm, factor_hbm, mixed_hbm, grad_hbm,
    back_ref, stream_ref, cot_ref, gain_ref, factor_ref, mixed_ref, moe_ref, sum_ref, sems, in_sems,
):
    packed = back_hbm.shape[1] // 2
    halves = [
        pltpu.make_async_copy(
            back_hbm.at[:, pl.ds(i * packed, packed)], back_ref.at[:, pl.ds(i * packed, packed)], sems.at[i]
        )
        for i in range(2)
    ]
    others = [
        pltpu.make_async_copy(source, target, in_sems.at[n])
        for n, (source, target) in enumerate(
            ((factor_hbm, factor_ref), (stream_hbm, stream_ref), (cot_hbm, cot_ref), (gain_hbm, gain_ref))
        )
    ]
    for one in others[:1] + halves[:1] + others[1:] + halves[1:]:
        one.start()
    width = stream_hbm.shape[1]
    part = width // 4
    rows = back_hbm.shape[0]
    others[0].wait()

    def weighted(n, rows_back):
        a = factor_ref[:, 2 * n * rows : (2 * n + 1) * rows]
        b = factor_ref[:, (2 * n + 1) * rows : (2 * n + 2) * rows]
        return dot(a, rows_back) + dot(b, rows_back)

    def gather(index, target):
        halves[index].wait()
        first = index * packed
        target[...] = weighted(0, back_ref[:, first : first + width])
        tail = back_ref[:, first + width : first + packed]
        for k in range(4):
            target[:, k * part : (k + 1) * part] += weighted(1 + k, tail)

    gather(0, moe_ref)
    for one in others[1:]:
        one.wait()
    stream = stream_ref[...]
    mixed_ref[...] = (stream + moe_ref[...]).astype(BF16)
    put_mixed = pltpu.make_async_copy(mixed_ref, mixed_hbm, sems.at[4])
    put_mixed.start()
    gather(1, sum_ref)
    scale_back = lax.rsqrt(jnp.mean(stream * stream, -1, keepdims=True) + 1e-06)
    gain_grad = gain_ref[...] * sum_ref[...]
    inner = jnp.mean(stream * gain_grad, -1, keepdims=True)
    moe_ref[...] = cot_ref[...].astype(F32) + scale_back * gain_grad - stream * (scale_back**3 * inner)
    put_grad = pltpu.make_async_copy(moe_ref, grad_hbm, sems.at[5])
    put_grad.start()
    put_mixed.wait()
    put_grad.wait()


def on_device(
    queries,
    key_rows,
    values,
    residual,
    seg_lengths,
    seg_parent,
    ln_gain,
    w_gate,
    w_up,
    w_down,
    expert_ids,
    gate_weights,
    cotangent,
):
    groups = lax.axis_size("exp")
    members = lax.axis_size("ctx")
    tokens, width = residual.shape[1], residual.shape[2]
    kv_width = key_rows.shape[2] + values.shape[2]
    hidden = w_gate.shape[2]
    slab = members * tokens
    rows = groups * BLOCK
    packed = width + width // 4
    shape = jax.ShapeDtypeStruct
    me = lax.axis_index("ctx").astype(jnp.int32).reshape(1)
    ids_t = expert_ids[0].T
    gain = ln_gain.reshape(1, width)

    in_smem = pl.BlockSpec(memory_space=pltpu.SMEM)
    anywhere = pl.BlockSpec(memory_space=pl.ANY)
    in_hbm = pl.BlockSpec(memory_space=pltpu.HBM)
    copy_sem = pltpu.SemaphoreType.DMA

    def tie(array, after):
        return pl.pallas_call(
            tie_body,
            out_shape=shape(array.shape, array.dtype),
            in_specs=[anywhere] * 2,
            out_specs=anywhere,
            input_output_aliases={0: 0},
        )(array, after)

    kv = call(
        pack_kv_body,
        shape((tokens, kv_width), BF16),
        [pltpu.VMEM((tokens, kv_width), BF16), copy_sem((3,))],
        [in_hbm] * 2,
        in_hbm,
    )(key_rows[0], values[0])
    w_own = call(
        pack_w_body,
        shape((tokens, 3 * hidden), BF16),
        [pltpu.VMEM(w_down.shape[1:], BF16), pltpu.VMEM((tokens, 3 * hidden), BF16), copy_sem((4,))],
        [in_hbm] * 3,
        in_hbm,
        moved=1 << 20,
    )(w_gate[0], w_up[0], w_down[0])

    def send(rows_out, target):
        return lax.ppermute(rows_out, "ctx", [(i, target(i)) for i in range(members)])

    def along_x(i, step):
        return (i // 4 + step) % 4 * 4 + i % 4

    def cross(rows_out):
        return send(rows_out, lambda i: i ^ 1)

    def stack(pieces, after=()):
        height = sum(piece.shape[0] for piece in pieces)
        return call(
            functools.partial(stack_body, len(pieces)),
            shape((height, pieces[0].shape[1]), BF16),
            [copy_sem((len(pieces),))],
            [in_hbm] * len(pieces) + [anywhere] * len(after),
            in_hbm,
            moved=2 * height * pieces[0].shape[1],
            vmem=ROOMY,
        )(*pieces, *after)

    factors = call(
        functools.partial(factor_body, groups),
        shape((tokens, 10 * rows), BF16),
        [
            pltpu.VMEM(ids_t.shape, jnp.int32),
            pltpu.VMEM(ids_t.shape, F32),
            pltpu.VMEM((tokens, 10 * rows), BF16),
            copy_sem((3,)),
        ],
        [in_hbm] * 2,
        in_hbm,
        moved=1 << 20,
    )(ids_t, gate_weights[0].T)
    bias = call(
        bias_body,
        shape((tokens, slab), F32),
        [
            pltpu.VMEM(seg_lengths.shape, jnp.int32),
            pltpu.VMEM(seg_parent.shape, jnp.int32),
            pltpu.VMEM((tokens, slab), F32),
            copy_sem((3,)),
        ],
        [in_smem] + [in_hbm] * 2,
        in_hbm,
        moved=1 << 20,
    )(me, seg_lengths, seg_parent)
    send_grad = call(
        functools.partial(scatter_body, groups),
        shape((rows, packed), BF16),
        [
            pltpu.VMEM((tokens, width), BF16),
            pltpu.VMEM(ids_t.shape, jnp.int32),
            pltpu.VMEM((rows, packed), BF16),
            copy_sem((3,)),
        ],
        [in_hbm] * 2,
        in_hbm,
        flops=2 * rows * tokens * width,
        moved=2 << 20,
    )(cotangent[0], ids_t)

    w_pair = send(w_own, lambda i: i ^ 2)
    kv_both = stack([kv, send(kv, lambda i: i ^ 2)])
    kv_near, kv_far, kv_last = (send(kv_both, functools.partial(along_x, step=step)) for step in (1, 2, 3))
    kv_mine = stack([kv_both, kv_near, kv_far, kv_last], [w_own, factors, bias])
    kv_core = cross(kv_mine)

    def exchange(sent):
        return lax.all_to_all(
            sent.reshape(groups, BLOCK, sent.shape[1]), "exp", split_axis=0, concat_axis=0, tiled=True
        ).reshape(sent.shape)

    arrived_grad = exchange(send_grad)
    stream, send_input = call(
        functools.partial(attend_body, groups),
        (shape((tokens, width), F32), shape((rows, packed), BF16)),
        [
            pltpu.VMEM((tokens, width), BF16),
            pltpu.VMEM((slab, kv_width), BF16),
            pltpu.VMEM((tokens, width), BF16),
            pltpu.VMEM((tokens, slab), F32),
            pltpu.VMEM((1, width), F32),
            pltpu.VMEM(ids_t.shape, jnp.int32),
            pltpu.VMEM((tokens, width), F32),
            pltpu.VMEM((rows, packed), BF16),
            copy_sem((9,)),
        ],
        [in_hbm] * 7,
        (in_hbm, in_hbm),
        flops=24 * tokens * slab * width,
        moved=8 << 20,
    )(queries[0], kv_mine, kv_core, residual[0], bias, gain, ids_t)
    send_input = tie(send_input, w_pair)
    arrived_in = exchange(send_input)
    w_both = stack([w_own, w_pair], [send_input])
    w_near = send(w_both, functools.partial(along_x, step=1))
    w_last = send(w_both, functools.partial(along_x, step=3))
    w_far_own = send(w_near[:tokens], functools.partial(along_x, step=1))
    w_far_pair = send(w_last[tokens:], functools.partial(along_x, step=3))
    w_pieces = [w_both, w_near, w_far_own, w_far_pair, w_last]
    w_pieces = w_pieces + [cross(piece) for piece in w_pieces]
    returned = call(
        expert_body,
        shape((rows, 2 * packed), BF16),
        [
            pltpu.VMEM((groups * CAP, width), BF16),
            pltpu.VMEM((rows, packed - width), BF16),
            pltpu.VMEM((groups * CAP, width), BF16),
            pltpu.VMEM((rows, packed - width), BF16),
            pltpu.VMEM((width, 3 * hidden), BF16),
            pltpu.VMEM((rows, 2 * packed), BF16),
            copy_sem((4,)),
            copy_sem((2, members)),
            copy_sem((2,)),
        ],
        [in_smem] + [in_hbm] * (2 + len(w_pieces)),
        in_hbm,
        flops=12 * groups * CAP * width * hidden,
        moved=10 << 20,
    )(me, arrived_in, arrived_grad, *w_pieces)
    back = exchange(returned)
    mixed_out, stream_grad = call(
        combine_body,
        (shape((tokens, width), BF16), shape((tokens, width), F32)),
        [
            pltpu.VMEM((rows, 2 * packed), BF16),
            pltpu.VMEM((tokens, width), F32),
            pltpu.VMEM((tokens, width), BF16),
            pltpu.VMEM((1, width), F32),
            pltpu.VMEM((tokens, 10 * rows), BF16),
            pltpu.VMEM((tokens, width), BF16),
            pltpu.VMEM((tokens, width), F32),
            pltpu.VMEM((tokens, width), F32),
            copy_sem((6,)),
            copy_sem((4,)),
        ],
        [in_hbm] * 5,
        (in_hbm, in_hbm),
    )(back, stream, cotangent[0], gain, factors)
    return (mixed_out[None], stream_grad[None])


def solution(mesh):
    placed = (
        P("exp", "ctx", None),
        P("exp", "ctx", None),
        P("exp", "ctx", None),
        P("exp", "ctx", None),
        P("exp", None),
        P("exp", None),
        P(),
        P("exp", "ctx", None),
        P("exp", "ctx", None),
        P("exp", None, "ctx"),
        P("exp", "ctx", None),
        P("exp", "ctx", None),
        P("exp", "ctx", None),
    )
    return jax.shard_map(
        on_device,
        mesh=mesh,
        in_specs=placed,
        out_specs=(P("exp", "ctx", None), P("exp", "ctx", None)),
        check_vma=False,
    )
```

time: 254 us -> 206 us (0.81)
  the two profiles are of different devices: /device:TPU:98 before, /device:TPU:56 now
where the time goes in v2:
time: 206 us; the launch traced here: 204 us
  blocking collectives  72 us (35%)
  starting transfers between devices  67.9 us (33%)
  Pallas kernels  39.1 us (19%)
  waiting for transfers between devices  19.2 us (9%)
  local copies, waits for them, and re-layouts  4.9 us (2%)
    all_to_all x1, blocking collectives, exchange(): lax.all_to_all(sent.reshape(groups, BLOCK, sent.shape[1]), 'exp', split_a...  72 us
    ppermute x15, starting transfers between devices, send(): lax.ppermute(rows_out, 'ctx', [(i, target(i)) for i in range(members)])  43.8 us
    all_to_all x2, starting transfers between devices, exchange(): lax.all_to_all(sent.reshape(groups, BLOCK, sent.shape[1]), 'exp', split_a...  24.1 us
    ppermute x15, waiting for transfers between devices, send(): lax.ppermute(rows_out, 'ctx', [(i, target(i)) for i in range(members)])  19.1 us
    pallas_call x1, Pallas kernels, on_device(): call(functools.partial(attend_body, groups), (shape((tokens, width), F32)...  11.5 us
    pallas_call x1, Pallas kernels, on_device(): call(expert_body, shape((rows, 2 * packed), BF16), [pltpu.VMEM((groups *...  10.3 us
    unnamed x36, local copies, waits for them, and re-layouts  4.86 us
    pallas_call x1, Pallas kernels, on_device(): call(combine_body, (shape((tokens, width), BF16), shape((tokens, width),...  4.68 us
  transfers between devices with their start and end apart: 17, of which 6 were waited for; matrix products, arithmetic and copies ran while one was open for 0% of the time, Pallas kernels for 11%

profile of v2, /device:TPU:56, one launch (start us, length us, event | category | flops | bytes accessed | tf_op | source)
XLA Modules:
  0.0 204.3 jit_solution(8323563740695844766)
XLA Ops:
  0.6 1.6 shard_map.140.refs_0_
  2.2 4.7 %collective-permute-start = (bf16[128,512]{1,0:T(8,128)(2,1)}, bf16[128,512]{1,0:T(8,128)(2,1)S(1)}, u32[]{:S(2)}, u32[]{:S(2)}) collective-permute-start(bf16[128,512]{1,0:T(8,128)(2,1)} %shard_map.140.refs_0_), channel_id=1, source_target_pairs={{0,64},{32,96},{64,0},{96,32},{128,192},{160,224},{192,128},{224,1... | collective-permute-start | bytes 393224 | tf_op jit(solution)/shard_map/ppermute | solution.py:460
  6.9 2.9 %shard_map.148 = bf16[256,2560]{1,0:T(8,128)(2,1)} custom-call(bf16[128,2048]{1,0:T(8,128)(2,1)} %bitcast.28, s32[8,128]{1,0:T(8,128)} %bitcast.36), custom_call_target="tpu_custom_call" | custom-call | flops 134217728 | bytes 2097152 | tf_op jit(solution)/shard_map/pallas_call | solution.py:506
  9.8 0.0 copy-start.7
  9.8 13.9 %all-to-all-start.1 = ((bf16[32,8,2560]{2,1,0:T(8,128)(2,1)}), bf16[32,8,2560]{2,1,0:T(8,128)(2,1)}, u32[]{:S(2)}, u32[]{:S(2)}) async-start(bf16[32,8,2560]{2,1,0:T(8,128)(2,1)} %bitcast.26), calls=%async_computation.1 | async-start | bytes 2621440 | tf_op jit(solution)/shard_map/all_to_all | solution.py:528
  23.7 0.0 collective-permute-done.refs_1_
  23.7 0.0 copy-done.7
  23.8 0.4 shard_map.141.refs_0_
  24.1 4.7 %collective-permute-start.3 = (bf16[256,512]{1,0:T(8,128)(2,1)S(1)}, bf16[256,512]{1,0:T(8,128)(2,1)S(1)}, u32[]{:S(2)}, u32[]{:S(2)}) collective-permute-start(bf16[256,512]{1,0:T(8,128)(2,1)S(1)} %shard_map.141.refs_0_), channel_id=1, source_target_pairs={{0,384},{32,416},{64,448},{96,480},{128,0},{160,32},{192,64},{224,... | collective-permute-start | bytes 786440 | tf_op jit(solution)/shard_map/ppermute | solution.py:460
  28.8 2.7 %collective-permute-start.2 = (bf16[256,512]{1,0:T(8,128)(2,1)S(1)}, bf16[256,512]{1,0:T(8,128)(2,1)S(1)}, u32[]{:S(2)}, u32[]{:S(2)}) collective-permute-start(bf16[256,512]{1,0:T(8,128)(2,1)S(1)} %shard_map.141.refs_0_), channel_id=1, source_target_pairs={{0,256},{32,288},{64,320},{96,352},{128,384},{160,416},{192,448},{... | collective-permute-start | bytes 786440 | tf_op jit(solution)/shard_map/ppermute | solution.py:460
  31.5 2.8 %collective-permute-start.1 = (bf16[256,512]{1,0:T(8,128)(2,1)S(1)}, bf16[256,512]{1,0:T(8,128)(2,1)S(1)}, u32[]{:S(2)}, u32[]{:S(2)}) collective-permute-start(bf16[256,512]{1,0:T(8,128)(2,1)S(1)} %shard_map.141.refs_0_), channel_id=1, source_target_pairs={{0,128},{32,160},{64,192},{96,224},{128,256},{160,288},{192,320},{... | collective-permute-start | bytes 786440 | tf_op jit(solution)/shard_map/ppermute | solution.py:460
  34.3 2.1 %shard_map.143.refs_5_.factor_hbm = bf16[128,2560]{1,0:T(8,128)(2,1)} custom-call(s32[8,128]{1,0:T(8,128)} %bitcast.37, f32[8,128]{1,0:T(8,128)} %bitcast.41), custom_call_target="tpu_custom_call" | custom-call | bytes 1048576 | tf_op jit(solution)/shard_map/pallas_call | solution.py:480
  36.4 0.0 copy-start.1
  36.4 1.9 shard_map.142.refs_4_.refs_0_
  38.3 2.7 %shard_map.144.refs_6_.bias_hbm = f32[128,2048]{1,0:T(8,128)} custom-call(s32[1]{0:T(128)} %bitcast.me_ref, s32[1,32]{1,0:T(1,128)} %len_hbm.1, s32[1,32]{1,0:T(1,128)} %parent_hbm.1), custom_call_target="tpu_custom_call" | custom-call | bytes 1048576 | tf_op jit(solution)/shard_map/pallas_call | solution.py:493
  41.1 0.0 collective-permute-done.3.refs_3_
  41.1 0.3 collective-permute-done.2.refs_2_
  41.4 3.3 %collective-permute-done.1.refs_1_ = bf16[256,512]{1,0:T(8,128)(2,1)S(1)} collective-permute-done((bf16[256,512]{1,0:T(8,128)(2,1)S(1)}, bf16[256,512]{1,0:T(8,128)(2,1)S(1)}, u32[]{:S(2)}, u32[]{:S(2)}) %collective-permute-start.1) | collective-permute-done | bytes 262176 | tf_op jit(solution)/shard_map/ppermute | solution.py:460
  44.7 0.0 copy-done.1
  44.7 1.2 copy-done.2
  46.0 0.1 shard_map.145.mine_hbm
  46.1 1.9 collective-permute-start.4
  48.0 5.0 %collective-permute-start.5 = (bf16[128,1152]{1,0:T(8,128)(2,1)}, bf16[128,1152]{1,0:T(8,128)(2,1)S(1)}, u32[]{:S(2)}, u32[]{:S(2)}) collective-permute-start(bf16[128,1152]{1,0:T(8,128)(2,1)} %shard_map.142.refs_4_.refs_0_), channel_id=1, source_target_pairs={{0,64},{32,96},{64,0},{96,32},{128,192},{160,224},{192,128},{224,1... | collective-permute-start | bytes 884744 | tf_op jit(solution)/shard_map/ppermute | solution.py:460
  53.1 0.0 collective-permute-done.4.core_hbm
  53.1 0.0 copy-start.11
  53.1 0.0 copy-done.5
  53.1 1.0 copy-done.11
  54.1 11.5 %shard_map.146 = (f32[128,2048]{1,0:T(8,128)}, bf16[256,2560]{1,0:T(8,128)(2,1)}) custom-call(bf16[128,2048]{1,0:T(8,128)(2,1)} %bitcast.43, bf16[1024,512]{1,0:T(8,128)(2,1)} %copy-done.5, bf16[1024,512]{1,0:T(8,128)(2,1)} %copy-done.11, bf16[128,2048]{1,0:T(8,128)(2,1)} %bitcast.44, f32[128,2048]{1,0:T(8,128)} %shard_map.144.refs_6_.bias_hbm, ...), custom_call_target="tpu_custom_call" | custom-call | flops 12884901888 | bytes 8388608 | tf_op jit(solution)/shard_map/pallas_call | solution.py:533
  65.6 4.2 %collective-permute-done.5.after_ref.refs_1_ = bf16[128,1152]{1,0:T(8,128)(2,1)S(1)} collective-permute-done((bf16[128,1152]{1,0:T(8,128)(2,1)}, bf16[128,1152]{1,0:T(8,128)(2,1)S(1)}, u32[]{:S(2)}, u32[]{:S(2)}) %collective-permute-start.5) | collective-permute-done | bytes 294944 | tf_op jit(solution)/shard_map/ppermute | solution.py:460
  69.8 0.7 copy-done.3
  70.5 0.0 all-to-all-done.1
  70.5 10.2 %all-to-all-start = ((bf16[32,8,2560]{2,1,0:T(8,128)(2,1)}), bf16[32,8,2560]{2,1,0:T(8,128)(2,1)S(1)}, u32[]{:S(2)}, u32[]{:S(2)}) async-start(bf16[32,8,2560]{2,1,0:T(8,128)(2,1)} %bitcast.24), calls=%async_computation | async-start | bytes 2621440 | tf_op jit(solution)/shard_map/all_to_all | solution.py:528
  80.7 1.0 shard_map.149.refs_0_
  81.7 0.0 copy-start.6
  81.7 2.5 %collective-permute-start.8 = (bf16[256,1152]{1,0:T(8,128)(2,1)S(1)}, bf16[256,1152]{1,0:T(8,128)(2,1)S(1)}, u32[]{:S(2)}, u32[]{:S(2)}) collective-permute-start(bf16[256,1152]{1,0:T(8,128)(2,1)S(1)} %shard_map.149.refs_0_), channel_id=1, source_target_pairs={{0,384},{32,416},{64,448},{96,480},{128,0},{160,32},{192,64},{224,... | collective-permute-start | bytes 1769480 | tf_op jit(solution)/shard_map/ppermute | solution.py:460
  84.2 3.4 %collective-permute-start.6 = (bf16[256,1152]{1,0:T(8,128)(2,1)S(1)}, bf16[256,1152]{1,0:T(8,128)(2,1)S(1)}, u32[]{:S(2)}, u32[]{:S(2)}) collective-permute-start(bf16[256,1152]{1,0:T(8,128)(2,1)S(1)} %shard_map.149.refs_0_), channel_id=1, source_target_pairs={{0,128},{32,160},{64,192},{96,224},{128,256},{160,288},{192,320},{... | collective-permute-start | bytes 1769480 | tf_op jit(solution)/shard_map/ppermute | solution.py:460
  87.6 1.9 collective-permute-start.10
  89.5 8.5 %collective-permute-done.8.refs_4_ = bf16[256,1152]{1,0:T(8,128)(2,1)S(1)} collective-permute-done((bf16[256,1152]{1,0:T(8,128)(2,1)S(1)}, bf16[256,1152]{1,0:T(8,128)(2,1)S(1)}, u32[]{:S(2)}, u32[]{:S(2)}) %collective-permute-start.8) | collective-permute-done | bytes 589856 | tf_op jit(solution)/shard_map/ppermute | solution.py:460
  98.0 3.7 %collective-permute-start.9 = (bf16[128,1152]{1,0:T(8,128)(2,1)S(1)}, bf16[128,1152]{1,0:T(8,128)(2,1)S(1)}, u32[]{:S(2)}, u32[]{:S(2)}) collective-permute-start(bf16[128,1152]{1,0:T(8,128)(2,1)S(1)} %slice.9), channel_id=1, source_target_pairs={{0,384},{32,416},{64,448},{96,480},{128,0},{160,32},{192,64},{224,... | collective-permute-start | bytes 884744 | tf_op jit(solution)/shard_map/ppermute | solution.py:460
  101.7 0.0 collective-permute-done.6.refs_1_
  101.8 2.2 %collective-permute-start.7 = (bf16[128,1152]{1,0:T(8,128)(2,1)S(1)}, bf16[128,1152]{1,0:T(8,128)(2,1)S(1)}, u32[]{:S(2)}, u32[]{:S(2)}) collective-permute-start(bf16[128,1152]{1,0:T(8,128)(2,1)S(1)} %slice.8), channel_id=1, source_target_pairs={{0,128},{32,160},{64,192},{96,224},{128,256},{160,288},{192,320},{... | collective-permute-start | bytes 884744 | tf_op jit(solution)/shard_map/ppermute | solution.py:460
  104.0 1.9 collective-permute-start.14
  105.9 2.4 %collective-permute-start.11 = (bf16[256,1152]{1,0:T(8,128)(2,1)S(1)}, bf16[256,1152]{1,0:T(8,128)(2,1)}, u32[]{:S(2)}, u32[]{:S(2)}) collective-permute-start(bf16[256,1152]{1,0:T(8,128)(2,1)S(1)} %collective-permute-done.6.refs_1_), channel_id=1, source_target_pairs={{0,32},{32,0},{64,96},{96,64},{128,160},{160,128},{192,224},{224,1... | collective-permute-start | bytes 1769480 | tf_op jit(solution)/shard_map/ppermute | solution.py:460
  108.3 0.0 collective-permute-done.9.refs_3_
  108.3 1.9 collective-permute-start.13
  110.3 1.5 collective-permute-done.7.refs_2_
  111.8 2.1 %collective-permute-start.12 = (bf16[128,1152]{1,0:T(8,128)(2,1)S(1)}, bf16[128,1152]{1,0:T(8,128)(2,1)S(1)}, u32[]{:S(2)}, u32[]{:S(2)}) collective-permute-start(bf16[128,1152]{1,0:T(8,128)(2,1)S(1)} %collective-permute-done.7.refs_2_), channel_id=1, source_target_pairs={{0,32},{32,0},{64,96},{96,64},{128,160},{160,128},{192,224},{224,1... | collective-permute-start | bytes 884744 | tf_op jit(solution)/shard_map/ppermute | solution.py:460
  113.9 0.0 collective-permute-done.10.refs_5_
  113.9 0.0 collective-permute-done.13.refs_8_
  113.9 1.3 collective-permute-done.12.refs_7_
  115.2 0.0 collective-permute-done.14.refs_9_
  115.2 0.0 copy-done.10
  115.3 0.9 copy-done.13
  116.2 0.0 collective-permute-done.11.refs_6_
  116.2 0.0 all-to-all-done
  116.2 0.0 copy-done.6
  116.2 0.0 copy-done.9
  116.2 0.0 copy-done.14
  116.2 0.0 copy-done.16
  116.2 0.0 copy-done.17
  116.2 1.0 copy-done.8
  117.2 10.3 %shard_map.150 = bf16[256,5120]{1,0:T(8,128)(2,1)} custom-call(s32[1]{0:T(128)} %bitcast.me_ref, bf16[256,2560]{1,0:T(8,128)(2,1)} %bitcast.30, bf16[256,2560]{1,0:T(8,128)(2,1)} %bitcast.18.grads_hbm, bf16[256,1152]{1,0:T(8,128)(2,1)} %copy-done.6, bf16[256,1152]{1,0:T(8,128)(2,1)} %copy-done.10, bf16[128,1152]{1,0:T(8,128)(2,1)} %copy-done.15, ...), custom_call_target="tpu_custom_call" | custom-call | flops 3019898880 | bytes 10485760 | tf_op jit(solution)/shard_map/pallas_call | solution.py:561
  127.5 72.0 %all_to_all.15 = bf16[32,8,5120]{2,1,0:T(8,128)(2,1)} all-to-all(bf16[32,8,5120]{2,1,0:T(8,128)(2,1)} %bitcast.27), channel_id=1, replica_groups=mesh['ctx'=16,'exp'=32] {'exp'}, dimensions={0} | all-to-all | bytes 5242880 | tf_op jit(solution)/shard_map/all_to_all | solution.py:528
  199.5 4.7 %shard_map.151 = (bf16[128,2048]{1,0:T(8,128)(2,1)}, f32[128,2048]{1,0:T(8,128)}) custom-call(bf16[256,5120]{1,0:T(8,128)(2,1)} %bitcast.25, f32[128,2048]{1,0:T(8,128)} %get-tuple-element.7.stream_hbm, bf16[128,2048]{1,0:T(8,128)(2,1)} %bitcast.29, f32[1,2048]{1,0:T(1,128)} %bitcast.40, bf16[128,2560]{1,0:T(8,128)(2,1)} %shard_map.143.refs_5_.factor_hbm), custom_call_target="tpu_custom_call" | custom-call | tf_op jit(solution)/shard_map/pallas_call | solution.py:581
  (21 shorter events, 0.1 us)
Async XLA Ops:
  2.2 21.5 %collective-permute-start = (bf16[128,512]{1,0:T(8,128)(2,1)}, bf16[128,512]{1,0:T(8,128)(2,1)S(1)}, u32[]{:S(2)}, u32[]{:S(2)}) collective-permute-start(bf16[128,512]{1,0:T(8,128)(2,1)} %shard_map.140.refs_0_), channel_id=1, source_target_pairs={{0,64},{32,96},{64,0},{96,32},{128,192},{160,224},{192,128},{224,1... | collective-permute-start | bytes 393224 | tf_op jit(solution)/shard_map/ppermute | solution.py:460
  9.8 14.0 %copy-start.7 = (bf16[128,512]{1,0:T(8,128)(2,1)S(1)}, bf16[128,512]{1,0:T(8,128)(2,1)}, u32[]{:S(2)}) copy-start(bf16[128,512]{1,0:T(8,128)(2,1)} %shard_map.140.refs_0_) | copy-start | bytes 393220
  9.8 60.7 %all-to-all-start.1 = ((bf16[32,8,2560]{2,1,0:T(8,128)(2,1)}), bf16[32,8,2560]{2,1,0:T(8,128)(2,1)}, u32[]{:S(2)}, u32[]{:S(2)}) async-start(bf16[32,8,2560]{2,1,0:T(8,128)(2,1)} %bitcast.26), calls=%async_computation.1 | async-start | bytes 2621440 | tf_op jit(solution)/shard_map/all_to_all | solution.py:528
  24.1 17.0 %collective-permute-start.3 = (bf16[256,512]{1,0:T(8,128)(2,1)S(1)}, bf16[256,512]{1,0:T(8,128)(2,1)S(1)}, u32[]{:S(2)}, u32[]{:S(2)}) collective-permute-start(bf16[256,512]{1,0:T(8,128)(2,1)S(1)} %shard_map.141.refs_0_), channel_id=1, source_target_pairs={{0,384},{32,416},{64,448},{96,480},{128,0},{160,32},{192,64},{224,... | collective-permute-start | bytes 786440 | tf_op jit(solution)/shard_map/ppermute | solution.py:460
  28.8 12.6 %collective-permute-start.2 = (bf16[256,512]{1,0:T(8,128)(2,1)S(1)}, bf16[256,512]{1,0:T(8,128)(2,1)S(1)}, u32[]{:S(2)}, u32[]{:S(2)}) collective-permute-start(bf16[256,512]{1,0:T(8,128)(2,1)S(1)} %shard_map.141.refs_0_), channel_id=1, source_target_pairs={{0,256},{32,288},{64,320},{96,352},{128,384},{160,416},{192,448},{... | collective-permute-start | bytes 786440 | tf_op jit(solution)/shard_map/ppermute | solution.py:460
  31.5 13.2 %collective-permute-start.1 = (bf16[256,512]{1,0:T(8,128)(2,1)S(1)}, bf16[256,512]{1,0:T(8,128)(2,1)S(1)}, u32[]{:S(2)}, u32[]{:S(2)}) collective-permute-start(bf16[256,512]{1,0:T(8,128)(2,1)S(1)} %shard_map.141.refs_0_), channel_id=1, source_target_pairs={{0,128},{32,160},{64,192},{96,224},{128,256},{160,288},{192,320},{... | collective-permute-start | bytes 786440 | tf_op jit(solution)/shard_map/ppermute | solution.py:460
  36.4 8.3 %copy-start.1 = (bf16[128,2560]{1,0:T(8,128)(2,1)S(1)}, bf16[128,2560]{1,0:T(8,128)(2,1)}, u32[]{:S(2)}) copy-start(bf16[128,2560]{1,0:T(8,128)(2,1)} %shard_map.143.refs_5_.factor_hbm) | copy-start | bytes 1966084
  44.7 1.2 copy-start.2
  46.1 7.0 %copy-start.5 = (bf16[1024,512]{1,0:T(8,128)(2,1)}, bf16[1024,512]{1,0:T(8,128)(2,1)S(1)}, u32[]{:S(2)}) copy-start(bf16[1024,512]{1,0:T(8,128)(2,1)S(1)} %shard_map.145.mine_hbm) | copy-start | bytes 3145732
  46.1 7.0 %collective-permute-start.4 = (bf16[1024,512]{1,0:T(8,128)(2,1)S(1)}, bf16[1024,512]{1,0:T(8,128)(2,1)S(1)}, u32[]{:S(2)}, u32[]{:S(2)}) collective-permute-start(bf16[1024,512]{1,0:T(8,128)(2,1)S(1)} %shard_map.145.mine_hbm), channel_id=1, source_target_pairs={{0,32},{32,0},{64,96},{96,64},{128,160},{160,128},{192,224},{224,1... | collective-permute-start | bytes 3145736 | tf_op jit(solution)/shard_map/ppermute | solution.py:460
  48.0 21.7 %collective-permute-start.5 = (bf16[128,1152]{1,0:T(8,128)(2,1)}, bf16[128,1152]{1,0:T(8,128)(2,1)S(1)}, u32[]{:S(2)}, u32[]{:S(2)}) collective-permute-start(bf16[128,1152]{1,0:T(8,128)(2,1)} %shard_map.142.refs_4_.refs_0_), channel_id=1, source_target_pairs={{0,64},{32,96},{64,0},{96,32},{128,192},{160,224},{192,128},{224,1... | collective-permute-start | bytes 884744 | tf_op jit(solution)/shard_map/ppermute | solution.py:460
  53.1 1.0 copy-start.11
  69.8 0.7 copy-start.3
  70.5 10.2 %copy-start = (bf16[256,2560]{1,0:T(8,128)(2,1)S(1)}, bf16[256,2560]{1,0:T(8,128)(2,1)}, u32[]{:S(2)}) copy-start(bf16[256,2560]{1,0:T(8,128)(2,1)} %shard_map.147.refs_2_) | copy-start | bytes 3932164
  70.5 10.2 %copy-start.4 = (bf16[128,1152]{1,0:T(8,128)(2,1)S(1)}, bf16[128,1152]{1,0:T(8,128)(2,1)}, u32[]{:S(2)}) copy-start(bf16[128,1152]{1,0:T(8,128)(2,1)} %copy-done.3) | copy-start | bytes 884740
  70.5 45.7 %all-to-all-start = ((bf16[32,8,2560]{2,1,0:T(8,128)(2,1)}), bf16[32,8,2560]{2,1,0:T(8,128)(2,1)S(1)}, u32[]{:S(2)}, u32[]{:S(2)}) async-start(bf16[32,8,2560]{2,1,0:T(8,128)(2,1)} %bitcast.24), calls=%async_computation | async-start | bytes 2621440 | tf_op jit(solution)/shard_map/all_to_all | solution.py:528
  81.7 34.4 %copy-start.6 = (bf16[256,1152]{1,0:T(8,128)(2,1)}, bf16[256,1152]{1,0:T(8,128)(2,1)S(1)}, u32[]{:S(2)}) copy-start(bf16[256,1152]{1,0:T(8,128)(2,1)S(1)} %shard_map.149.refs_0_) | copy-start | bytes 1769476
  81.7 16.3 %collective-permute-start.8 = (bf16[256,1152]{1,0:T(8,128)(2,1)S(1)}, bf16[256,1152]{1,0:T(8,128)(2,1)S(1)}, u32[]{:S(2)}, u32[]{:S(2)}) collective-permute-start(bf16[256,1152]{1,0:T(8,128)(2,1)S(1)} %shard_map.149.refs_0_), channel_id=1, source_target_pairs={{0,384},{32,416},{64,448},{96,480},{128,0},{160,32},{192,64},{224,... | collective-permute-start | bytes 1769480 | tf_op jit(solution)/shard_map/ppermute | solution.py:460
  84.2 17.5 %collective-permute-start.6 = (bf16[256,1152]{1,0:T(8,128)(2,1)S(1)}, bf16[256,1152]{1,0:T(8,128)(2,1)S(1)}, u32[]{:S(2)}, u32[]{:S(2)}) collective-permute-start(bf16[256,1152]{1,0:T(8,128)(2,1)S(1)} %shard_map.149.refs_0_), channel_id=1, source_target_pairs={{0,128},{32,160},{64,192},{96,224},{128,256},{160,288},{192,320},{... | collective-permute-start | bytes 1769480 | tf_op jit(solution)/shard_map/ppermute | solution.py:460
  87.6 26.3 %collective-permute-start.10 = (bf16[256,1152]{1,0:T(8,128)(2,1)S(1)}, bf16[256,1152]{1,0:T(8,128)(2,1)S(1)}, u32[]{:S(2)}, u32[]{:S(2)}) collective-permute-start(bf16[256,1152]{1,0:T(8,128)(2,1)S(1)} %shard_map.149.refs_0_), channel_id=1, source_target_pairs={{0,32},{32,0},{64,96},{96,64},{128,160},{160,128},{192,224},{224,1... | collective-permute-start | bytes 1769480 | tf_op jit(solution)/shard_map/ppermute | solution.py:460
  98.0 18.2 %copy-start.9 = (bf16[256,1152]{1,0:T(8,128)(2,1)}, bf16[256,1152]{1,0:T(8,128)(2,1)S(1)}, u32[]{:S(2)}) copy-start(bf16[256,1152]{1,0:T(8,128)(2,1)S(1)} %collective-permute-done.8.refs_4_) | copy-start | bytes 1769476
  98.0 10.3 %collective-permute-start.9 = (bf16[128,1152]{1,0:T(8,128)(2,1)S(1)}, bf16[128,1152]{1,0:T(8,128)(2,1)S(1)}, u32[]{:S(2)}, u32[]{:S(2)}) collective-permute-start(bf16[128,1152]{1,0:T(8,128)(2,1)S(1)} %slice.9), channel_id=1, source_target_pairs={{0,384},{32,416},{64,448},{96,480},{128,0},{160,32},{192,64},{224,... | collective-permute-start | bytes 884744 | tf_op jit(solution)/shard_map/ppermute | solution.py:460
  101.7 13.5 %copy-start.10 = (bf16[256,1152]{1,0:T(8,128)(2,1)}, bf16[256,1152]{1,0:T(8,128)(2,1)S(1)}, u32[]{:S(2)}) copy-start(bf16[256,1152]{1,0:T(8,128)(2,1)S(1)} %collective-permute-done.6.refs_1_) | copy-start | bytes 1769476
  101.8 10.0 %collective-permute-start.7 = (bf16[128,1152]{1,0:T(8,128)(2,1)S(1)}, bf16[128,1152]{1,0:T(8,128)(2,1)S(1)}, u32[]{:S(2)}, u32[]{:S(2)}) collective-permute-start(bf16[128,1152]{1,0:T(8,128)(2,1)S(1)} %slice.8), channel_id=1, source_target_pairs={{0,128},{32,160},{64,192},{96,224},{128,256},{160,288},{192,320},{... | collective-permute-start | bytes 884744 | tf_op jit(solution)/shard_map/ppermute | solution.py:460
  104.0 11.3 %collective-permute-start.14 = (bf16[256,1152]{1,0:T(8,128)(2,1)S(1)}, bf16[256,1152]{1,0:T(8,128)(2,1)S(1)}, u32[]{:S(2)}, u32[]{:S(2)}) collective-permute-start(bf16[256,1152]{1,0:T(8,128)(2,1)S(1)} %collective-permute-done.8.refs_4_), channel_id=1, source_target_pairs={{0,32},{32,0},{64,96},{96,64},{128,160},{160,128},{192,224},{224,1... | collective-permute-start | bytes 1769480 | tf_op jit(solution)/shard_map/ppermute | solution.py:460
  105.9 10.3 %collective-permute-start.11 = (bf16[256,1152]{1,0:T(8,128)(2,1)S(1)}, bf16[256,1152]{1,0:T(8,128)(2,1)}, u32[]{:S(2)}, u32[]{:S(2)}) collective-permute-start(bf16[256,1152]{1,0:T(8,128)(2,1)S(1)} %collective-permute-done.6.refs_1_), channel_id=1, source_target_pairs={{0,32},{32,0},{64,96},{96,64},{128,160},{160,128},{192,224},{224,1... | collective-permute-start | bytes 1769480 | tf_op jit(solution)/shard_map/ppermute | solution.py:460
  108.3 7.9 %copy-start.14 = (bf16[128,1152]{1,0:T(8,128)(2,1)}, bf16[128,1152]{1,0:T(8,128)(2,1)S(1)}, u32[]{:S(2)}) copy-start(bf16[128,1152]{1,0:T(8,128)(2,1)S(1)} %collective-permute-done.9.refs_3_) | copy-start | bytes 884740
  108.3 5.6 %collective-permute-start.13 = (bf16[128,1152]{1,0:T(8,128)(2,1)S(1)}, bf16[128,1152]{1,0:T(8,128)(2,1)S(1)}, u32[]{:S(2)}, u32[]{:S(2)}) collective-permute-start(bf16[128,1152]{1,0:T(8,128)(2,1)S(1)} %collective-permute-done.9.refs_3_), channel_id=1, source_target_pairs={{0,32},{32,0},{64,96},{96,64},{128,160},{160,128},{192,224},{224,1... | collective-permute-start | bytes 884744 | tf_op jit(solution)/shard_map/ppermute | solution.py:460
  111.8 3.5 %copy-start.15 = (bf16[128,1152]{1,0:T(8,128)(2,1)}, bf16[128,1152]{1,0:T(8,128)(2,1)S(1)}, u32[]{:S(2)}) copy-start(bf16[128,1152]{1,0:T(8,128)(2,1)S(1)} %collective-permute-done.7.refs_2_) | copy-start | bytes 884740
  111.8 3.5 %collective-permute-start.12 = (bf16[128,1152]{1,0:T(8,128)(2,1)S(1)}, bf16[128,1152]{1,0:T(8,128)(2,1)S(1)}, u32[]{:S(2)}, u32[]{:S(2)}) collective-permute-start(bf16[128,1152]{1,0:T(8,128)(2,1)S(1)} %collective-permute-done.7.refs_2_), channel_id=1, source_target_pairs={{0,32},{32,0},{64,96},{96,64},{128,160},{160,128},{192,224},{224,1... | collective-permute-start | bytes 884744 | tf_op jit(solution)/shard_map/ppermute | solution.py:460
  113.9 1.4 copy-start.12
  113.9 2.3 %copy-start.16 = (bf16[128,1152]{1,0:T(8,128)(2,1)}, bf16[128,1152]{1,0:T(8,128)(2,1)S(1)}, u32[]{:S(2)}) copy-start(bf16[128,1152]{1,0:T(8,128)(2,1)S(1)} %collective-permute-done.13.refs_8_) | copy-start | bytes 884740
  115.2 1.0 copy-start.17
  115.3 0.9 copy-start.13
  116.2 1.1 copy-start.8

commit v3 on v2

--- a/solution.py
+++ b/solution.py
@@ -13,7 +13,7 @@
 CAP = 10
 BLOCK = 8
 NO_SLOT = 512.0
-TOGETHER = 4
+TOGETHER = 8
 ROOMY = 28 << 20
 ALONE = 60 << 20
 HIDDEN = -1e30
@@ -118,10 +118,6 @@
     copy_all(copies)
 
 
-def tie_body(array_ref, after_ref, out_ref):
-    del array_ref, after_ref, out_ref
-
-
 def scatter_body(groups, rows_hbm, ids_hbm, send_hbm, rows_ref, ids_ref, send_ref, sems):
     get_ids = pltpu.make_async_copy(ids_hbm, ids_ref, sems.at[0])
     get_rows = pltpu.make_async_copy(rows_hbm, rows_ref, sems.at[1])
@@ -134,7 +130,7 @@
     copy_all([pltpu.make_async_copy(send_ref, send_hbm, sems.at[2])])
 
 
-def bias_body(me_ref, len_hbm, parent_hbm, bias_hbm, len_ref, parent_ref, bias_ref, sems):
+def bias_body(me_ref, len_hbm, parent_hbm, bias_hbm, len_ref, parent_ref, bias_ref, sems, put_sem):
     copy_all(
         [
             pltpu.make_async_copy(len_hbm, len_ref, sems.at[0]),
@@ -165,7 +161,9 @@
         linked = dot(query_reach, holds.astype(BF16))
         visible = (linked > 0.5) & (key_pos <= query_pos)
         bias_ref[:, n * rows : (n + 1) * rows] = jnp.where(visible, 0.0, HIDDEN)
-    copy_all([pltpu.make_async_copy(bias_ref, bias_hbm, sems.at[2])])
+    put = pltpu.make_async_copy(bias_ref, bias_hbm, put_sem.at[0])
+    put.start()
+    return put
 
 
 def attend_body(
@@ -268,7 +266,7 @@
     get_grads = fetch_rows(grads_hbm, g_ref, g_tail, 2)
     get_in = fetch_weights(0, 0, 2 * hidden)
     get_out = fetch_weights(1, 2 * hidden, hidden)
-    for one in get_rows + get_in + get_out + get_grads:
+    for one in get_grads + get_out + get_rows + get_in:
         one.start()
 
     def unpack(tail, target):
@@ -291,6 +289,12 @@
         copy.start()
         return copy
 
+    for one in get_grads:
+        one.wait()
+    unpack(g_tail, g_ref)
+    for one in get_out:
+        one.wait()
+    back = dot(g_ref[...], w_ref[:, 2 * hidden :])
     for one in get_rows:
         one.wait()
     unpack(x_tail, x_ref)
@@ -301,16 +305,10 @@
     sig = jax.nn.sigmoid(gate)
     silu = gate * sig
     activated = (silu * up).astype(BF16)
-    for one in get_out:
-        one.wait()
     put_out = pack(dot_nt(activated, w_ref[:, 2 * hidden :]).astype(BF16), 0)
-    for one in get_grads:
-        one.wait()
-    unpack(g_tail, g_ref)
-    back = dot(g_ref[...], w_ref[:, 2 * hidden :])
     d_gate = (back * up * sig * (1.0 + gate * (1.0 - sig))).astype(BF16)
     d_up = (back * silu).astype(BF16)
-    grad = dot_nt(d_gate, w_ref[:, :hidden]) + dot_nt(d_up, w_ref[:, hidden : 2 * hidden])
+    grad = dot_nt(jnp.concatenate([d_gate, d_up], 1), w_ref[:, : 2 * hidden])
     put_grad = pack(grad.astype(BF16), 1)
     put_out.wait()
     put_grad.wait()
@@ -341,6 +339,18 @@
         factor_ref[:, 2 * n * rows : (2 * n + 1) * rows] = jnp.where(mask, coarse, 0.0).astype(BF16)
         factor_ref[:, (2 * n + 1) * rows : (2 * n + 2) * rows] = jnp.where(mask, fine, 0.0).astype(BF16)
     copy_all([pltpu.make_async_copy(factor_ref, factor_hbm, sems.at[2])])
+
+
+def tables_body(
+    groups, me_ref, len_hbm, parent_hbm, ids_hbm, weight_hbm, gate_hbm, up_hbm, down_hbm,
+    w_hbm, bias_hbm, factor_hbm,
+    len_ref, parent_ref, bias_ref, ids_ref, weight_ref, factor_ref, down_ref, w_ref,
+    bias_sems, factor_sems, put_sem, w_sems,
+):
+    put = bias_body(me_ref, len_hbm, parent_hbm, bias_hbm, len_ref, parent_ref, bias_ref, bias_sems, put_sem)
+    factor_body(groups, ids_hbm, weight_hbm, factor_hbm, ids_ref, weight_ref, factor_ref, factor_sems)
+    pack_w_body(gate_hbm, up_hbm, down_hbm, w_hbm, down_ref, w_ref, w_sems)
+    put.wait()
 
 
 def combine_body(
@@ -431,15 +441,6 @@
     in_hbm = pl.BlockSpec(memory_space=pltpu.HBM)
     copy_sem = pltpu.SemaphoreType.DMA
 
-    def tie(array, after):
-        return pl.pallas_call(
-            tie_body,
-            out_shape=shape(array.shape, array.dtype),
-            in_specs=[anywhere] * 2,
-            out_specs=anywhere,
-            input_output_aliases={0: 0},
-        )(array, after)
-
     kv = call(
         pack_kv_body,
         shape((tokens, kv_width), BF16),
@@ -447,15 +448,6 @@
         [in_hbm] * 2,
         in_hbm,
     )(key_rows[0], values[0])
-    w_own = call(
-        pack_w_body,
-        shape((tokens, 3 * hidden), BF16),
-        [pltpu.VMEM(w_down.shape[1:], BF16), pltpu.VMEM((tokens, 3 * hidden), BF16), copy_sem((4,))],
-        [in_hbm] * 3,
-        in_hbm,
-        moved=1 << 20,
-    )(w_gate[0], w_up[0], w_down[0])
-
     def send(rows_out, target):
         return lax.ppermute(rows_out, "ctx", [(i, target(i)) for i in range(members)])
 
@@ -465,7 +457,7 @@
     def cross(rows_out):
         return send(rows_out, lambda i: i ^ 1)
 
-    def stack(pieces, after=()):
+    def stack(pieces, after=(), flops=0):
         height = sum(piece.shape[0] for piece in pieces)
         return call(
             functools.partial(stack_body, len(pieces)),
@@ -473,36 +465,32 @@
             [copy_sem((len(pieces),))],
             [in_hbm] * len(pieces) + [anywhere] * len(after),
             in_hbm,
-            moved=2 * height * pieces[0].shape[1],
+            flops=flops,
+            moved=1 << 20,
             vmem=ROOMY,
         )(*pieces, *after)
 
-    factors = call(
-        functools.partial(factor_body, groups),
-        shape((tokens, 10 * rows), BF16),
-        [
-            pltpu.VMEM(ids_t.shape, jnp.int32),
-            pltpu.VMEM(ids_t.shape, F32),
-            pltpu.VMEM((tokens, 10 * rows), BF16),
-            copy_sem((3,)),
-        ],
-        [in_hbm] * 2,
-        in_hbm,
-        moved=1 << 20,
-    )(ids_t, gate_weights[0].T)
-    bias = call(
-        bias_body,
-        shape((tokens, slab), F32),
+    w_own, bias, factors = call(
+        functools.partial(tables_body, groups),
+        (shape((tokens, 3 * hidden), BF16), shape((tokens, slab), F32), shape((tokens, 10 * rows), BF16)),
         [
             pltpu.VMEM(seg_lengths.shape, jnp.int32),
             pltpu.VMEM(seg_parent.shape, jnp.int32),
             pltpu.VMEM((tokens, slab), F32),
+            pltpu.VMEM(ids_t.shape, jnp.int32),
+            pltpu.VMEM(ids_t.shape, F32),
+            pltpu.VMEM((tokens, 10 * rows), BF16),
+            pltpu.VMEM(w_down.shape[1:], BF16),
+            pltpu.VMEM((tokens, 3 * hidden), BF16),
+            copy_sem((2,)),
             copy_sem((3,)),
+            copy_sem((1,)),
+            copy_sem((4,)),
         ],
-        [in_smem] + [in_hbm] * 2,
-        in_hbm,
-        moved=1 << 20,
-    )(me, seg_lengths, seg_parent)
+        [in_smem] + [in_hbm] * 7,
+        (in_hbm, in_hbm, in_hbm),
+        moved=2 << 20,
+    )(me, seg_lengths, seg_parent, ids_t, gate_weights[0].T, w_gate[0], w_up[0], w_down[0])
     send_grad = call(
         functools.partial(scatter_body, groups),
         shape((rows, packed), BF16),
@@ -521,7 +509,7 @@
     w_pair = send(w_own, lambda i: i ^ 2)
     kv_both = stack([kv, send(kv, lambda i: i ^ 2)])
     kv_near, kv_far, kv_last = (send(kv_both, functools.partial(along_x, step=step)) for step in (1, 2, 3))
-    kv_mine = stack([kv_both, kv_near, kv_far, kv_last], [w_own, factors, bias])
+    kv_mine = stack([kv_both, kv_near, kv_far, kv_last], [w_own])
     kv_core = cross(kv_mine)
 
     def exchange(sent):
@@ -546,12 +534,12 @@
         ],
         [in_hbm] * 7,
         (in_hbm, in_hbm),
+        vmem=62 << 20,
         flops=24 * tokens * slab * width,
         moved=8 << 20,
     )(queries[0], kv_mine, kv_core, residual[0], bias, gain, ids_t)
-    send_input = tie(send_input, w_pair)
     arrived_in = exchange(send_input)
-    w_both = stack([w_own, w_pair], [send_input])
+    w_both = stack([w_own, w_pair], [send_input], 16 << 30)
     w_near = send(w_both, functools.partial(along_x, step=1))
     w_last = send(w_both, functools.partial(along_x, step=3))
     w_far_own = send(w_near[:tokens], functools.partial(along_x, step=1))

time: 206 us -> 199 us (0.966)
  Pallas kernels: 39.1 us -> 36.7 us
  local copies, waits for them, and re-layouts: 4.9 us -> 2.72 us
    unnamed x36 -> x28, local copies, waits for them, and re-layouts: 4.86 us -> 2.67 us
    pallas_call x4 -> x1, Pallas kernels: 6.74 us -> 5.43 us  [on_device(): call(functools.partial(tables_body, groups), (shape((tokens, 3 * hidden),...]
  transfers between devices with their start and end apart: 17 -> 17, of which waited for: 6 -> 5; matrix products, arithmetic and copies ran while one was open for 0% -> 0% of each run, Pallas kernels for 11% -> 10%
where the time goes in v3:
time: 199 us; the launch traced here: 198 us
  blocking collectives  71.9 us (36%)
  starting transfers between devices  68 us (34%)
  Pallas kernels  36.7 us (18%)
  waiting for transfers between devices  17.5 us (9%)
  local copies, waits for them, and re-layouts  2.72 us (1%)
    all_to_all x1, blocking collectives, exchange(): lax.all_to_all(sent.reshape(groups, BLOCK, sent.shape[1]), 'exp', split_a...  71.9 us
    ppermute x15, starting transfers between devices, send(): lax.ppermute(rows_out, 'ctx', [(i, target(i)) for i in range(members)])  43.8 us
    all_to_all x2, starting transfers between devices, exchange(): lax.all_to_all(sent.reshape(groups, BLOCK, sent.shape[1]), 'exp', split_a...  24.2 us
    ppermute x15, waiting for transfers between devices, send(): lax.ppermute(rows_out, 'ctx', [(i, target(i)) for i in range(members)])  17.5 us
    pallas_call x1, Pallas kernels, on_device(): call(functools.partial(attend_body, groups), (shape((tokens, width), F32)...  11 us
    pallas_call x1, Pallas kernels, on_device(): call(expert_body, shape((rows, 2 * packed), BF16), [pltpu.VMEM((groups *...  9.72 us
    pallas_call x1, Pallas kernels, on_device(): call(functools.partial(tables_body, groups), (shape((tokens, 3 * hidden),...  5.43 us
    pallas_call x1, Pallas kernels, on_device(): call(combine_body, (shape((tokens, width), BF16), shape((tokens, width),...  4.68 us
  transfers between devices with their start and end apart: 17, of which 5 were waited for; matrix products, arithmetic and copies ran while one was open for 0% of the time, Pallas kernels for 10%

profile of v3, /device:TPU:56, one launch (start us, length us, event | category | flops | bytes accessed | tf_op | source)
XLA Modules:
  0.0 198.0 jit_solution(15601334239703990875)
XLA Ops:
  0.6 1.6 shard_map.140.refs_0_
  2.2 4.7 %collective-permute-start = (bf16[128,512]{1,0:T(8,128)(2,1)}, bf16[128,512]{1,0:T(8,128)(2,1)S(1)}, u32[]{:S(2)}, u32[]{:S(2)}) collective-permute-start(bf16[128,512]{1,0:T(8,128)(2,1)} %shard_map.140.refs_0_), channel_id=1, source_target_pairs={{0,64},{32,96},{64,0},{96,32},{128,192},{160,224},{192,128},{224,1... | collective-permute-start | bytes 393224 | tf_op jit(solution)/shard_map/ppermute | solution.py:452
  6.9 2.9 %shard_map.145 = bf16[256,2560]{1,0:T(8,128)(2,1)} custom-call(bf16[128,2048]{1,0:T(8,128)(2,1)} %bitcast.28, s32[8,128]{1,0:T(8,128)} %bitcast.35), custom_call_target="tpu_custom_call" | custom-call | flops 134217728 | bytes 2097152 | tf_op jit(solution)/shard_map/pallas_call | solution.py:494
  9.8 0.0 copy-start.2
  9.8 13.9 %all-to-all-start.1 = ((bf16[32,8,2560]{2,1,0:T(8,128)(2,1)}), bf16[32,8,2560]{2,1,0:T(8,128)(2,1)}, u32[]{:S(2)}, u32[]{:S(2)}) async-start(bf16[32,8,2560]{2,1,0:T(8,128)(2,1)} %bitcast.26), calls=%async_computation.1 | async-start | bytes 2621440 | tf_op jit(solution)/shard_map/all_to_all | solution.py:516
  23.7 0.0 collective-permute-done.refs_1_
  23.7 0.0 copy-done.2
  23.7 0.4 shard_map.141.refs_0_
  24.1 4.7 %collective-permute-start.3 = (bf16[256,512]{1,0:T(8,128)(2,1)S(1)}, bf16[256,512]{1,0:T(8,128)(2,1)S(1)}, u32[]{:S(2)}, u32[]{:S(2)}) collective-permute-start(bf16[256,512]{1,0:T(8,128)(2,1)S(1)} %shard_map.141.refs_0_), channel_id=1, source_target_pairs={{0,384},{32,416},{64,448},{96,480},{128,0},{160,32},{192,64},{224,... | collective-permute-start | bytes 786440 | tf_op jit(solution)/shard_map/ppermute | solution.py:452
  28.8 2.7 %collective-permute-start.2 = (bf16[256,512]{1,0:T(8,128)(2,1)S(1)}, bf16[256,512]{1,0:T(8,128)(2,1)S(1)}, u32[]{:S(2)}, u32[]{:S(2)}) collective-permute-start(bf16[256,512]{1,0:T(8,128)(2,1)S(1)} %shard_map.141.refs_0_), channel_id=1, source_target_pairs={{0,256},{32,288},{64,320},{96,352},{128,384},{160,416},{192,448},{... | collective-permute-start | bytes 786440 | tf_op jit(solution)/shard_map/ppermute | solution.py:452
  31.5 2.8 %collective-permute-start.1 = (bf16[256,512]{1,0:T(8,128)(2,1)S(1)}, bf16[256,512]{1,0:T(8,128)(2,1)S(1)}, u32[]{:S(2)}, u32[]{:S(2)}) collective-permute-start(bf16[256,512]{1,0:T(8,128)(2,1)S(1)} %shard_map.141.refs_0_), channel_id=1, source_target_pairs={{0,128},{32,160},{64,192},{96,224},{128,256},{160,288},{192,320},{... | collective-permute-start | bytes 786440 | tf_op jit(solution)/shard_map/ppermute | solution.py:452
  34.3 5.4 %shard_map.142 = (bf16[128,1152]{1,0:T(8,128)(2,1)}, f32[128,2048]{1,0:T(8,128)}, bf16[128,2560]{1,0:T(8,128)(2,1)}) custom-call(s32[1]{0:T(128)} %bitcast.me_ref, s32[1,32]{1,0:T(1,128)} %len_hbm.1, s32[1,32]{1,0:T(1,128)} %parent_hbm.1, s32[8,128]{1,0:T(8,128)} %bitcast.36, f32[8,128]{1,0:T(8,128)} %bitcast.40, bf16[128,384]{1,0:T(8,128)(2,1)} %bitcast.30, ...), custom_call_target="tpu_custom_call" | custom-call | bytes 2097152 | tf_op jit(solution)/shard_map/pallas_call | solution.py:473
  39.8 0.0 collective-permute-done.3.refs_3_
  39.8 1.7 collective-permute-done.2.refs_2_
  41.4 3.3 %collective-permute-done.1.refs_1_ = bf16[256,512]{1,0:T(8,128)(2,1)S(1)} collective-permute-done((bf16[256,512]{1,0:T(8,128)(2,1)S(1)}, bf16[256,512]{1,0:T(8,128)(2,1)S(1)}, u32[]{:S(2)}, u32[]{:S(2)}) %collective-permute-start.1) | collective-permute-done | bytes 262176 | tf_op jit(solution)/shard_map/ppermute | solution.py:452
  44.7 0.1 shard_map.143.mine_hbm
  44.9 0.0 copy-start.1
  44.9 1.9 collective-permute-start.4
  46.8 5.0 %collective-permute-start.5 = (bf16[128,1152]{1,0:T(8,128)(2,1)}, bf16[128,1152]{1,0:T(8,128)(2,1)S(1)}, u32[]{:S(2)}, u32[]{:S(2)}) collective-permute-start(bf16[128,1152]{1,0:T(8,128)(2,1)} %get-tuple-element.9.refs_4_.refs_0_), channel_id=1, source_target_pairs={{0,64},{32,96},{64,0},{96,32},{128,192},{160,224},{192,128},{224,1... | collective-permute-start | bytes 884744 | tf_op jit(solution)/shard_map/ppermute | solution.py:452
  51.8 0.0 collective-permute-done.4.core_hbm
  51.8 0.0 copy-start.6
  51.9 1.0 copy-done.6
  52.8 0.0 copy-done.1
  52.8 11.0 %shard_map.144 = (f32[128,2048]{1,0:T(8,128)}, bf16[256,2560]{1,0:T(8,128)(2,1)}) custom-call(bf16[128,2048]{1,0:T(8,128)(2,1)} %bitcast.42, bf16[1024,512]{1,0:T(8,128)(2,1)} %copy-done.1, bf16[1024,512]{1,0:T(8,128)(2,1)} %copy-done.6, bf16[128,2048]{1,0:T(8,128)(2,1)} %bitcast.43, f32[128,2048]{1,0:T(8,128)} %get-tuple-element.10.bias_hbm, ...), custom_call_target="tpu_custom_call" | custom-call | flops 12884901888 | bytes 8388608 | tf_op jit(solution)/shard_map/pallas_call | solution.py:521
  63.9 0.0 all-to-all-done.1
  63.9 0.0 copy-start
  63.9 10.3 %all-to-all-start = ((bf16[32,8,2560]{2,1,0:T(8,128)(2,1)}), bf16[32,8,2560]{2,1,0:T(8,128)(2,1)}, u32[]{:S(2)}, u32[]{:S(2)}) async-start(bf16[32,8,2560]{2,1,0:T(8,128)(2,1)} %bitcast.24), calls=%async_computation | async-start | bytes 2621440 | tf_op jit(solution)/shard_map/all_to_all | solution.py:516
  74.2 0.0 collective-permute-done.5.refs_1_
  74.2 0.0 copy-done
  74.2 1.0 shard_map.146.refs_0_
  75.2 0.0 copy-start.3
  75.2 2.5 %collective-permute-start.8 = (bf16[256,1152]{1,0:T(8,128)(2,1)S(1)}, bf16[256,1152]{1,0:T(8,128)(2,1)S(1)}, u32[]{:S(2)}, u32[]{:S(2)}) collective-permute-start(bf16[256,1152]{1,0:T(8,128)(2,1)S(1)} %shard_map.146.refs_0_), channel_id=1, source_target_pairs={{0,384},{32,416},{64,448},{96,480},{128,0},{160,32},{192,64},{224,... | collective-permute-start | bytes 1769480 | tf_op jit(solution)/shard_map/ppermute | solution.py:452
  77.7 3.4 %collective-permute-start.6 = (bf16[256,1152]{1,0:T(8,128)(2,1)S(1)}, bf16[256,1152]{1,0:T(8,128)(2,1)S(1)}, u32[]{:S(2)}, u32[]{:S(2)}) collective-permute-start(bf16[256,1152]{1,0:T(8,128)(2,1)S(1)} %shard_map.146.refs_0_), channel_id=1, source_target_pairs={{0,128},{32,160},{64,192},{96,224},{128,256},{160,288},{192,320},{... | collective-permute-start | bytes 1769480 | tf_op jit(solution)/shard_map/ppermute | solution.py:452
  81.0 1.9 collective-permute-start.10
  83.0 9.0 %collective-permute-done.8.refs_4_ = bf16[256,1152]{1,0:T(8,128)(2,1)S(1)} collective-permute-done((bf16[256,1152]{1,0:T(8,128)(2,1)S(1)}, bf16[256,1152]{1,0:T(8,128)(2,1)S(1)}, u32[]{:S(2)}, u32[]{:S(2)}) %collective-permute-start.8) | collective-permute-done | bytes 589856 | tf_op jit(solution)/shard_map/ppermute | solution.py:452
  92.0 3.7 %collective-permute-start.9 = (bf16[128,1152]{1,0:T(8,128)(2,1)S(1)}, bf16[128,1152]{1,0:T(8,128)(2,1)S(1)}, u32[]{:S(2)}, u32[]{:S(2)}) collective-permute-start(bf16[128,1152]{1,0:T(8,128)(2,1)S(1)} %slice.9), channel_id=1, source_target_pairs={{0,384},{32,416},{64,448},{96,480},{128,0},{160,32},{192,64},{224,... | collective-permute-start | bytes 884744 | tf_op jit(solution)/shard_map/ppermute | solution.py:452
  95.7 0.0 collective-permute-done.6.refs_1_
  95.7 0.0 copy-start.5
  95.7 2.2 %collective-permute-start.7 = (bf16[128,1152]{1,0:T(8,128)(2,1)S(1)}, bf16[128,1152]{1,0:T(8,128)(2,1)S(1)}, u32[]{:S(2)}, u32[]{:S(2)}) collective-permute-start(bf16[128,1152]{1,0:T(8,128)(2,1)S(1)} %slice.8), channel_id=1, source_target_pairs={{0,128},{32,160},{64,192},{96,224},{128,256},{160,288},{192,320},{... | collective-permute-start | bytes 884744 | tf_op jit(solution)/shard_map/ppermute | solution.py:452
  97.9 1.9 collective-permute-start.14
  99.8 2.4 %collective-permute-start.11 = (bf16[256,1152]{1,0:T(8,128)(2,1)S(1)}, bf16[256,1152]{1,0:T(8,128)(2,1)S(1)}, u32[]{:S(2)}, u32[]{:S(2)}) collective-permute-start(bf16[256,1152]{1,0:T(8,128)(2,1)S(1)} %collective-permute-done.6.refs_1_), channel_id=1, source_target_pairs={{0,32},{32,0},{64,96},{96,64},{128,160},{160,128},{192,224},{224,1... | collective-permute-start | bytes 1769480 | tf_op jit(solution)/shard_map/ppermute | solution.py:452
  102.2 0.0 collective-permute-done.9.refs_3_
  102.3 0.0 copy-start.10
  102.3 2.1 %collective-permute-start.13 = (bf16[128,1152]{1,0:T(8,128)(2,1)S(1)}, bf16[128,1152]{1,0:T(8,128)(2,1)S(1)}, u32[]{:S(2)}, u32[]{:S(2)}) collective-permute-start(bf16[128,1152]{1,0:T(8,128)(2,1)S(1)} %collective-permute-done.9.refs_3_), channel_id=1, source_target_pairs={{0,32},{32,0},{64,96},{96,64},{128,160},{160,128},{192,224},{224,1... | collective-permute-start | bytes 884744 | tf_op jit(solution)/shard_map/ppermute | solution.py:452
  104.4 2.0 collective-permute-done.7.refs_2_
  106.3 1.9 collective-permute-start.12
  108.3 0.0 collective-permute-done.10.refs_5_
  108.3 0.0 copy-start.7
  108.3 0.0 collective-permute-done.13.refs_8_
  108.3 0.0 copy-start.12
  108.3 1.5 collective-permute-done.12.refs_7_
  109.8 0.0 collective-permute-done.14.refs_9_
  109.8 0.0 copy-done.10
  109.8 0.0 copy-done.11
  109.8 0.0 copy-done.12
  109.8 0.7 copy-done.13
  110.5 0.0 collective-permute-done.11.refs_6_
  110.5 0.0 all-to-all-done
  110.5 0.0 copy-done.3
  110.6 0.8 copy-done.8
  111.3 0.2 copy-done.9
  111.5 9.7 %shard_map.147 = bf16[256,5120]{1,0:T(8,128)(2,1)} custom-call(s32[1]{0:T(128)} %bitcast.me_ref, bf16[256,2560]{1,0:T(8,128)(2,1)} %bitcast.14.rows_hbm, bf16[256,2560]{1,0:T(8,128)(2,1)} %bitcast.18.grads_hbm, bf16[256,1152]{1,0:T(8,128)(2,1)} %copy-done.3, bf16[256,1152]{1,0:T(8,128)(2,1)} %copy-done.5, bf16[128,1152]{1,0:T(8,128)(2,1)} %copy-done.11, ...), custom_call_target="tpu_custom_call" | custom-call | flops 3019898880 | bytes 10485760 | tf_op jit(solution)/shard_map/pallas_call | solution.py:549
  121.3 71.9 %all_to_all.15 = bf16[32,8,5120]{2,1,0:T(8,128)(2,1)} all-to-all(bf16[32,8,5120]{2,1,0:T(8,128)(2,1)} %bitcast.27), channel_id=1, replica_groups=mesh['ctx'=16,'exp'=32] {'exp'}, dimensions={0} | all-to-all | bytes 5242880 | tf_op jit(solution)/shard_map/all_to_all | solution.py:516
  193.2 4.7 %shard_map.148 = (bf16[128,2048]{1,0:T(8,128)(2,1)}, f32[128,2048]{1,0:T(8,128)}) custom-call(bf16[256,5120]{1,0:T(8,128)(2,1)} %bitcast.25, f32[128,2048]{1,0:T(8,128)} %get-tuple-element.12.stream_hbm, bf16[128,2048]{1,0:T(8,128)(2,1)} %bitcast.29, f32[1,2048]{1,0:T(1,128)} %bitcast.39, bf16[128,2560]{1,0:T(8,128)(2,1)} %get-tuple-element.13.factor_hbm), custom_call_target="tpu_custom_call" | custom-call | tf_op jit(solution)/shard_map/pallas_call | solution.py:569
  (10 shorter events, 0.1 us)
Async XLA Ops:
  2.2 21.5 %collective-permute-start = (bf16[128,512]{1,0:T(8,128)(2,1)}, bf16[128,512]{1,0:T(8,128)(2,1)S(1)}, u32[]{:S(2)}, u32[]{:S(2)}) collective-permute-start(bf16[128,512]{1,0:T(8,128)(2,1)} %shard_map.140.refs_0_), channel_id=1, source_target_pairs={{0,64},{32,96},{64,0},{96,32},{128,192},{160,224},{192,128},{224,1... | collective-permute-start | bytes 393224 | tf_op jit(solution)/shard_map/ppermute | solution.py:452
  9.8 14.0 %copy-start.2 = (bf16[128,512]{1,0:T(8,128)(2,1)S(1)}, bf16[128,512]{1,0:T(8,128)(2,1)}, u32[]{:S(2)}) copy-start(bf16[128,512]{1,0:T(8,128)(2,1)} %shard_map.140.refs_0_) | copy-start | bytes 393220
  9.8 54.1 %all-to-all-start.1 = ((bf16[32,8,2560]{2,1,0:T(8,128)(2,1)}), bf16[32,8,2560]{2,1,0:T(8,128)(2,1)}, u32[]{:S(2)}, u32[]{:S(2)}) async-start(bf16[32,8,2560]{2,1,0:T(8,128)(2,1)} %bitcast.26), calls=%async_computation.1 | async-start | bytes 2621440 | tf_op jit(solution)/shard_map/all_to_all | solution.py:516
  24.1 15.6 %collective-permute-start.3 = (bf16[256,512]{1,0:T(8,128)(2,1)S(1)}, bf16[256,512]{1,0:T(8,128)(2,1)S(1)}, u32[]{:S(2)}, u32[]{:S(2)}) collective-permute-start(bf16[256,512]{1,0:T(8,128)(2,1)S(1)} %shard_map.141.refs_0_), channel_id=1, source_target_pairs={{0,384},{32,416},{64,448},{96,480},{128,0},{160,32},{192,64},{224,... | collective-permute-start | bytes 786440 | tf_op jit(solution)/shard_map/ppermute | solution.py:452
  28.8 12.6 %collective-permute-start.2 = (bf16[256,512]{1,0:T(8,128)(2,1)S(1)}, bf16[256,512]{1,0:T(8,128)(2,1)S(1)}, u32[]{:S(2)}, u32[]{:S(2)}) collective-permute-start(bf16[256,512]{1,0:T(8,128)(2,1)S(1)} %shard_map.141.refs_0_), channel_id=1, source_target_pairs={{0,256},{32,288},{64,320},{96,352},{128,384},{160,416},{192,448},{... | collective-permute-start | bytes 786440 | tf_op jit(solution)/shard_map/ppermute | solution.py:452
  31.5 13.2 %collective-permute-start.1 = (bf16[256,512]{1,0:T(8,128)(2,1)S(1)}, bf16[256,512]{1,0:T(8,128)(2,1)S(1)}, u32[]{:S(2)}, u32[]{:S(2)}) collective-permute-start(bf16[256,512]{1,0:T(8,128)(2,1)S(1)} %shard_map.141.refs_0_), channel_id=1, source_target_pairs={{0,128},{32,160},{64,192},{96,224},{128,256},{160,288},{192,320},{... | collective-permute-start | bytes 786440 | tf_op jit(solution)/shard_map/ppermute | solution.py:452
  44.9 8.0 %copy-start.1 = (bf16[1024,512]{1,0:T(8,128)(2,1)}, bf16[1024,512]{1,0:T(8,128)(2,1)S(1)}, u32[]{:S(2)}) copy-start(bf16[1024,512]{1,0:T(8,128)(2,1)S(1)} %shard_map.143.mine_hbm) | copy-start | bytes 3145732
  44.9 7.0 %collective-permute-start.4 = (bf16[1024,512]{1,0:T(8,128)(2,1)S(1)}, bf16[1024,512]{1,0:T(8,128)(2,1)S(1)}, u32[]{:S(2)}, u32[]{:S(2)}) collective-permute-start(bf16[1024,512]{1,0:T(8,128)(2,1)S(1)} %shard_map.143.mine_hbm), channel_id=1, source_target_pairs={{0,32},{32,0},{64,96},{96,64},{128,160},{160,128},{192,224},{224,1... | collective-permute-start | bytes 3145736 | tf_op jit(solution)/shard_map/ppermute | solution.py:452
  46.8 27.4 %collective-permute-start.5 = (bf16[128,1152]{1,0:T(8,128)(2,1)}, bf16[128,1152]{1,0:T(8,128)(2,1)S(1)}, u32[]{:S(2)}, u32[]{:S(2)}) collective-permute-start(bf16[128,1152]{1,0:T(8,128)(2,1)} %get-tuple-element.9.refs_4_.refs_0_), channel_id=1, source_target_pairs={{0,64},{32,96},{64,0},{96,32},{128,192},{160,224},{192,128},{224,1... | collective-permute-start | bytes 884744 | tf_op jit(solution)/shard_map/ppermute | solution.py:452
  51.8 1.0 copy-start.6
  63.9 10.3 %copy-start = (bf16[256,2560]{1,0:T(8,128)(2,1)S(1)}, bf16[256,2560]{1,0:T(8,128)(2,1)}, u32[]{:S(2)}) copy-start(bf16[256,2560]{1,0:T(8,128)(2,1)} %get-tuple-element.11.refs_2_) | copy-start | bytes 3932164
  63.9 46.6 %all-to-all-start = ((bf16[32,8,2560]{2,1,0:T(8,128)(2,1)}), bf16[32,8,2560]{2,1,0:T(8,128)(2,1)}, u32[]{:S(2)}, u32[]{:S(2)}) async-start(bf16[32,8,2560]{2,1,0:T(8,128)(2,1)} %bitcast.24), calls=%async_computation | async-start | bytes 2621440 | tf_op jit(solution)/shard_map/all_to_all | solution.py:516
  75.2 35.4 %copy-start.3 = (bf16[256,1152]{1,0:T(8,128)(2,1)}, bf16[256,1152]{1,0:T(8,128)(2,1)S(1)}, u32[]{:S(2)}) copy-start(bf16[256,1152]{1,0:T(8,128)(2,1)S(1)} %shard_map.146.refs_0_) | copy-start | bytes 1769476
  75.2 16.8 %collective-permute-start.8 = (bf16[256,1152]{1,0:T(8,128)(2,1)S(1)}, bf16[256,1152]{1,0:T(8,128)(2,1)S(1)}, u32[]{:S(2)}, u32[]{:S(2)}) collective-permute-start(bf16[256,1152]{1,0:T(8,128)(2,1)S(1)} %shard_map.146.refs_0_), channel_id=1, source_target_pairs={{0,384},{32,416},{64,448},{96,480},{128,0},{160,32},{192,64},{224,... | collective-permute-start | bytes 1769480 | tf_op jit(solution)/shard_map/ppermute | solution.py:452
  77.7 18.0 %collective-permute-start.6 = (bf16[256,1152]{1,0:T(8,128)(2,1)S(1)}, bf16[256,1152]{1,0:T(8,128)(2,1)S(1)}, u32[]{:S(2)}, u32[]{:S(2)}) collective-permute-start(bf16[256,1152]{1,0:T(8,128)(2,1)S(1)} %shard_map.146.refs_0_), channel_id=1, source_target_pairs={{0,128},{32,160},{64,192},{96,224},{128,256},{160,288},{192,320},{... | collective-permute-start | bytes 1769480 | tf_op jit(solution)/shard_map/ppermute | solution.py:452
  81.0 27.2 %collective-permute-start.10 = (bf16[256,1152]{1,0:T(8,128)(2,1)S(1)}, bf16[256,1152]{1,0:T(8,128)(2,1)S(1)}, u32[]{:S(2)}, u32[]{:S(2)}) collective-permute-start(bf16[256,1152]{1,0:T(8,128)(2,1)S(1)} %shard_map.146.refs_0_), channel_id=1, source_target_pairs={{0,32},{32,0},{64,96},{96,64},{128,160},{160,128},{192,224},{224,1... | collective-permute-start | bytes 1769480 | tf_op jit(solution)/shard_map/ppermute | solution.py:452
  92.0 18.6 %copy-start.4 = (bf16[256,1152]{1,0:T(8,128)(2,1)}, bf16[256,1152]{1,0:T(8,128)(2,1)S(1)}, u32[]{:S(2)}) copy-start(bf16[256,1152]{1,0:T(8,128)(2,1)S(1)} %collective-permute-done.8.refs_4_) | copy-start | bytes 1769476
  92.0 10.3 %collective-permute-start.9 = (bf16[128,1152]{1,0:T(8,128)(2,1)S(1)}, bf16[128,1152]{1,0:T(8,128)(2,1)S(1)}, u32[]{:S(2)}, u32[]{:S(2)}) collective-permute-start(bf16[128,1152]{1,0:T(8,128)(2,1)S(1)} %slice.9), channel_id=1, source_target_pairs={{0,384},{32,416},{64,448},{96,480},{128,0},{160,32},{192,64},{224,... | collective-permute-start | bytes 884744 | tf_op jit(solution)/shard_map/ppermute | solution.py:452
  95.7 14.9 %copy-start.5 = (bf16[256,1152]{1,0:T(8,128)(2,1)}, bf16[256,1152]{1,0:T(8,128)(2,1)S(1)}, u32[]{:S(2)}) copy-start(bf16[256,1152]{1,0:T(8,128)(2,1)S(1)} %collective-permute-done.6.refs_1_) | copy-start | bytes 1769476
  95.7 10.6 %collective-permute-start.7 = (bf16[128,1152]{1,0:T(8,128)(2,1)S(1)}, bf16[128,1152]{1,0:T(8,128)(2,1)S(1)}, u32[]{:S(2)}, u32[]{:S(2)}) collective-permute-start(bf16[128,1152]{1,0:T(8,128)(2,1)S(1)} %slice.8), channel_id=1, source_target_pairs={{0,128},{32,160},{64,192},{96,224},{128,256},{160,288},{192,320},{... | collective-permute-start | bytes 884744 | tf_op jit(solution)/shard_map/ppermute | solution.py:452
  97.9 11.9 %collective-permute-start.14 = (bf16[256,1152]{1,0:T(8,128)(2,1)S(1)}, bf16[256,1152]{1,0:T(8,128)(2,1)S(1)}, u32[]{:S(2)}, u32[]{:S(2)}) collective-permute-start(bf16[256,1152]{1,0:T(8,128)(2,1)S(1)} %collective-permute-done.8.refs_4_), channel_id=1, source_target_pairs={{0,32},{32,0},{64,96},{96,64},{128,160},{160,128},{192,224},{224,1... | collective-permute-start | bytes 1769480 | tf_op jit(solution)/shard_map/ppermute | solution.py:452
  99.8 10.7 %collective-permute-start.11 = (bf16[256,1152]{1,0:T(8,128)(2,1)S(1)}, bf16[256,1152]{1,0:T(8,128)(2,1)S(1)}, u32[]{:S(2)}, u32[]{:S(2)}) collective-permute-start(bf16[256,1152]{1,0:T(8,128)(2,1)S(1)} %collective-permute-done.6.refs_1_), channel_id=1, source_target_pairs={{0,32},{32,0},{64,96},{96,64},{128,160},{160,128},{192,224},{224,1... | collective-permute-start | bytes 1769480 | tf_op jit(solution)/shard_map/ppermute | solution.py:452
  102.3 7.6 %copy-start.10 = (bf16[128,1152]{1,0:T(8,128)(2,1)}, bf16[128,1152]{1,0:T(8,128)(2,1)S(1)}, u32[]{:S(2)}) copy-start(bf16[128,1152]{1,0:T(8,128)(2,1)S(1)} %collective-permute-done.9.refs_3_) | copy-start | bytes 884740
  102.3 6.0 %collective-permute-start.13 = (bf16[128,1152]{1,0:T(8,128)(2,1)S(1)}, bf16[128,1152]{1,0:T(8,128)(2,1)S(1)}, u32[]{:S(2)}, u32[]{:S(2)}) collective-permute-start(bf16[128,1152]{1,0:T(8,128)(2,1)S(1)} %collective-permute-done.9.refs_3_), channel_id=1, source_target_pairs={{0,32},{32,0},{64,96},{96,64},{128,160},{160,128},{192,224},{224,1... | collective-permute-start | bytes 884744 | tf_op jit(solution)/shard_map/ppermute | solution.py:452
  106.3 3.5 %copy-start.11 = (bf16[128,1152]{1,0:T(8,128)(2,1)}, bf16[128,1152]{1,0:T(8,128)(2,1)S(1)}, u32[]{:S(2)}) copy-start(bf16[128,1152]{1,0:T(8,128)(2,1)S(1)} %collective-permute-done.7.refs_2_) | copy-start | bytes 884740
  106.3 3.5 %collective-permute-start.12 = (bf16[128,1152]{1,0:T(8,128)(2,1)S(1)}, bf16[128,1152]{1,0:T(8,128)(2,1)S(1)}, u32[]{:S(2)}, u32[]{:S(2)}) collective-permute-start(bf16[128,1152]{1,0:T(8,128)(2,1)S(1)} %collective-permute-done.7.refs_2_), channel_id=1, source_target_pairs={{0,32},{32,0},{64,96},{96,64},{128,160},{160,128},{192,224},{224,1... | collective-permute-start | bytes 884744 | tf_op jit(solution)/shard_map/ppermute | solution.py:452
  108.3 2.3 %copy-start.7 = (bf16[256,1152]{1,0:T(8,128)(2,1)}, bf16[256,1152]{1,0:T(8,128)(2,1)S(1)}, u32[]{:S(2)}) copy-start(bf16[256,1152]{1,0:T(8,128)(2,1)S(1)} %collective-permute-done.10.refs_5_) | copy-start | bytes 1769476
  108.3 1.5 copy-start.12
  109.8 0.7 copy-start.13
  110.5 0.8 copy-start.8
  110.5 1.0 copy-start.9

commit v4 on v3

--- a/solution.py
+++ b/solution.py
@@ -60,18 +60,23 @@
     return dot(spread.astype(BF16), key)
 
 
-def dispatch(rows, keys, out_ref):
+def dispatch(rows, keys, out_ref, out_hbm, sems):
     place = iota(keys.shape, 0)
     width = rows.shape[1]
     part = width // 4
+    columns = pl.ds(0, width), pl.ds(width, part)
+    copies = [pltpu.make_async_copy(out_ref.at[:, c], out_hbm.at[:, c], sems.at[n]) for n, c in enumerate(columns)]
     pick = jnp.where(keys == (place % BLOCK).astype(F32), 1.0, 0.0).astype(BF16)
     out_ref[:, :width] = dot(pick, rows).astype(BF16)
+    copies[0].start()
     late = keys == (BLOCK + (place % BLOCK) // 4).astype(F32)
     tail = jnp.zeros((keys.shape[0], part), F32)
     for k in range(4):
         pick = jnp.where(late & (place % 4 == k), 1.0, 0.0).astype(BF16)
         tail = tail + dot(pick, rows[:, k * part : (k + 1) * part])
     out_ref[:, width:] = tail.astype(BF16)
+    copies[1].start()
+    return copies
 
 
 def copy_all(copies):
@@ -118,7 +123,7 @@
     copy_all(copies)
 
 
-def scatter_body(groups, rows_hbm, ids_hbm, send_hbm, rows_ref, ids_ref, send_ref, sems):
+def scatter_body(groups, rows_hbm, ids_hbm, send_hbm, rows_ref, ids_ref, send_ref, sems, out_sems):
     get_ids = pltpu.make_async_copy(ids_hbm, ids_ref, sems.at[0])
     get_rows = pltpu.make_async_copy(rows_hbm, rows_ref, sems.at[1])
     get_ids.start()
@@ -126,8 +131,8 @@
     get_ids.wait()
     keys = slot_keys(ids_ref[...], groups)
     get_rows.wait()
-    dispatch(rows_ref[...], keys, send_ref)
-    copy_all([pltpu.make_async_copy(send_ref, send_hbm, sems.at[2])])
+    for one in dispatch(rows_ref[...], keys, send_ref, send_hbm, out_sems):
+        one.wait()
 
 
 def bias_body(me_ref, len_hbm, parent_hbm, bias_hbm, len_ref, parent_ref, bias_ref, sems, put_sem):
@@ -186,6 +191,7 @@
     stream_ref,
     send_ref,
     sems,
+    out_sems,
 ):
     pieces, first, fetch = (mine_hbm, core_hbm), 0, []
     for n, piece in enumerate(pieces):
@@ -229,11 +235,8 @@
     keep.start()
     scale_back = lax.rsqrt(jnp.mean(stream * stream, -1, keepdims=True) + 1e-06)
     normed = (stream * scale_back * gain_ref[...]).astype(BF16)
-    dispatch(normed, slot_keys(ids_ref[...], groups), send_ref)
-    out = pltpu.make_async_copy(send_ref, send_hbm, sems.at[5])
-    out.start()
-    keep.wait()
-    out.wait()
+    for one in dispatch(normed, slot_keys(ids_ref[...], groups), send_ref, send_hbm, out_sems) + [keep]:
+        one.wait()
 
 
 def expert_body(me_ref, rows_hbm, grads_hbm, *refs):
@@ -498,7 +501,8 @@
             pltpu.VMEM((tokens, width), BF16),
             pltpu.VMEM(ids_t.shape, jnp.int32),
             pltpu.VMEM((rows, packed), BF16),
-            copy_sem((3,)),
+            copy_sem((2,)),
+            copy_sem((2,)),
         ],
         [in_hbm] * 2,
         in_hbm,
@@ -531,6 +535,7 @@
             pltpu.VMEM((tokens, width), F32),
             pltpu.VMEM((rows, packed), BF16),
             copy_sem((9,)),
+            copy_sem((2,)),
         ],
         [in_hbm] * 7,
         (in_hbm, in_hbm),

time: 199 us -> 199 us (level)
  no operation moved by 1% of the time
where the time goes in v4:
time: 199 us; the launch traced here: 198 us
  blocking collectives  72 us (36%)
  starting transfers between devices  68 us (34%)
  Pallas kernels  36.3 us (18%)
  waiting for transfers between devices  17.5 us (9%)
  local copies, waits for them, and re-layouts  2.72 us (1%)
    all_to_all x1, blocking collectives, exchange(): lax.all_to_all(sent.reshape(groups, BLOCK, sent.shape[1]), 'exp', split_a...  72 us
    ppermute x15, starting transfers between devices, send(): lax.ppermute(rows_out, 'ctx', [(i, target(i)) for i in range(members)])  43.8 us
    all_to_all x2, starting transfers between devices, exchange(): lax.all_to_all(sent.reshape(groups, BLOCK, sent.shape[1]), 'exp', split_a...  24.2 us
    ppermute x15, waiting for transfers between devices, send(): lax.ppermute(rows_out, 'ctx', [(i, target(i)) for i in range(members)])  17.4 us
    pallas_call x1, Pallas kernels, on_device(): call(functools.partial(attend_body, groups), (shape((tokens, width), F32)...  10.8 us
    pallas_call x1, Pallas kernels, on_device(): call(expert_body, shape((rows, 2 * packed), BF16), [pltpu.VMEM((groups *...  9.72 us
    pallas_call x1, Pallas kernels, on_device(): call(functools.partial(tables_body, groups), (shape((tokens, 3 * hidden),...  5.44 us
    pallas_call x1, Pallas kernels, on_device(): call(combine_body, (shape((tokens, width), BF16), shape((tokens, width),...  4.68 us
  transfers between devices with their start and end apart: 17, of which 5 were waited for; matrix products, arithmetic and copies ran while one was open for 0% of the time, Pallas kernels for 10%

profile of v4, /device:TPU:56, one launch (start us, length us, event | category | flops | bytes accessed | tf_op | source)
XLA Modules:
  0.0 197.6 jit_solution(6384306994981755649)
XLA Ops:
  0.6 1.6 shard_map.140.refs_0_
  2.2 4.7 %collective-permute-start = (bf16[128,512]{1,0:T(8,128)(2,1)}, bf16[128,512]{1,0:T(8,128)(2,1)S(1)}, u32[]{:S(2)}, u32[]{:S(2)}) collective-permute-start(bf16[128,512]{1,0:T(8,128)(2,1)} %shard_map.140.refs_0_), channel_id=1, source_target_pairs={{0,64},{32,96},{64,0},{96,32},{128,192},{160,224},{192,128},{224,1... | collective-permute-start | bytes 393224 | tf_op jit(solution)/shard_map/ppermute | solution.py:455
  6.9 2.7 %shard_map.145 = bf16[256,2560]{1,0:T(8,128)(2,1)} custom-call(bf16[128,2048]{1,0:T(8,128)(2,1)} %bitcast.28, s32[8,128]{1,0:T(8,128)} %bitcast.35), custom_call_target="tpu_custom_call" | custom-call | flops 134217728 | bytes 2097152 | tf_op jit(solution)/shard_map/pallas_call | solution.py:497
  9.6 0.0 copy-start.2
  9.6 13.9 %all-to-all-start.1 = ((bf16[32,8,2560]{2,1,0:T(8,128)(2,1)}), bf16[32,8,2560]{2,1,0:T(8,128)(2,1)}, u32[]{:S(2)}, u32[]{:S(2)}) async-start(bf16[32,8,2560]{2,1,0:T(8,128)(2,1)} %bitcast.26), calls=%async_computation.1 | async-start | bytes 2621440 | tf_op jit(solution)/shard_map/all_to_all | solution.py:520
  23.5 0.0 collective-permute-done.refs_1_
  23.5 0.0 copy-done.2
  23.5 0.4 shard_map.141.refs_0_
  23.9 4.7 %collective-permute-start.3 = (bf16[256,512]{1,0:T(8,128)(2,1)S(1)}, bf16[256,512]{1,0:T(8,128)(2,1)S(1)}, u32[]{:S(2)}, u32[]{:S(2)}) collective-permute-start(bf16[256,512]{1,0:T(8,128)(2,1)S(1)} %shard_map.141.refs_0_), channel_id=1, source_target_pairs={{0,384},{32,416},{64,448},{96,480},{128,0},{160,32},{192,64},{224,... | collective-permute-start | bytes 786440 | tf_op jit(solution)/shard_map/ppermute | solution.py:455
  28.6 2.7 %collective-permute-start.2 = (bf16[256,512]{1,0:T(8,128)(2,1)S(1)}, bf16[256,512]{1,0:T(8,128)(2,1)S(1)}, u32[]{:S(2)}, u32[]{:S(2)}) collective-permute-start(bf16[256,512]{1,0:T(8,128)(2,1)S(1)} %shard_map.141.refs_0_), channel_id=1, source_target_pairs={{0,256},{32,288},{64,320},{96,352},{128,384},{160,416},{192,448},{... | collective-permute-start | bytes 786440 | tf_op jit(solution)/shard_map/ppermute | solution.py:455
  31.3 2.8 %collective-permute-start.1 = (bf16[256,512]{1,0:T(8,128)(2,1)S(1)}, bf16[256,512]{1,0:T(8,128)(2,1)S(1)}, u32[]{:S(2)}, u32[]{:S(2)}) collective-permute-start(bf16[256,512]{1,0:T(8,128)(2,1)S(1)} %shard_map.141.refs_0_), channel_id=1, source_target_pairs={{0,128},{32,160},{64,192},{96,224},{128,256},{160,288},{192,320},{... | collective-permute-start | bytes 786440 | tf_op jit(solution)/shard_map/ppermute | solution.py:455
  34.1 5.4 %shard_map.142 = (bf16[128,1152]{1,0:T(8,128)(2,1)}, f32[128,2048]{1,0:T(8,128)}, bf16[128,2560]{1,0:T(8,128)(2,1)}) custom-call(s32[1]{0:T(128)} %bitcast.me_ref, s32[1,32]{1,0:T(1,128)} %len_hbm.1, s32[1,32]{1,0:T(1,128)} %parent_hbm.1, s32[8,128]{1,0:T(8,128)} %bitcast.36, f32[8,128]{1,0:T(8,128)} %bitcast.40, bf16[128,384]{1,0:T(8,128)(2,1)} %bitcast.30, ...), custom_call_target="tpu_custom_call" | custom-call | bytes 2097152 | tf_op jit(solution)/shard_map/pallas_call | solution.py:476
  39.5 0.0 collective-permute-done.3.refs_3_
  39.5 1.7 collective-permute-done.2.refs_2_
  41.2 3.3 %collective-permute-done.1.refs_1_ = bf16[256,512]{1,0:T(8,128)(2,1)S(1)} collective-permute-done((bf16[256,512]{1,0:T(8,128)(2,1)S(1)}, bf16[256,512]{1,0:T(8,128)(2,1)S(1)}, u32[]{:S(2)}, u32[]{:S(2)}) %collective-permute-start.1) | collective-permute-done | bytes 262176 | tf_op jit(solution)/shard_map/ppermute | solution.py:455
  44.5 0.1 shard_map.143.mine_hbm
  44.6 0.0 copy-start.1
  44.6 1.9 collective-permute-start.4
  46.6 5.0 %collective-permute-start.5 = (bf16[128,1152]{1,0:T(8,128)(2,1)}, bf16[128,1152]{1,0:T(8,128)(2,1)S(1)}, u32[]{:S(2)}, u32[]{:S(2)}) collective-permute-start(bf16[128,1152]{1,0:T(8,128)(2,1)} %get-tuple-element.9.refs_4_.refs_0_), channel_id=1, source_target_pairs={{0,64},{32,96},{64,0},{96,32},{128,192},{160,224},{192,128},{224,1... | collective-permute-start | bytes 884744 | tf_op jit(solution)/shard_map/ppermute | solution.py:455
  51.6 0.0 collective-permute-done.4.core_hbm
  51.6 0.0 copy-start.6
  51.6 1.0 copy-done.6
  52.6 0.0 copy-done.1
  52.6 10.8 %shard_map.144 = (f32[128,2048]{1,0:T(8,128)}, bf16[256,2560]{1,0:T(8,128)(2,1)}) custom-call(bf16[128,2048]{1,0:T(8,128)(2,1)} %bitcast.42, bf16[1024,512]{1,0:T(8,128)(2,1)} %copy-done.1, bf16[1024,512]{1,0:T(8,128)(2,1)} %copy-done.6, bf16[128,2048]{1,0:T(8,128)(2,1)} %bitcast.43, f32[128,2048]{1,0:T(8,128)} %get-tuple-element.10.bias_hbm, ...), custom_call_target="tpu_custom_call" | custom-call | flops 12884901888 | bytes 8388608 | tf_op jit(solution)/shard_map/pallas_call | solution.py:525
  63.4 0.0 all-to-all-done.1
  63.4 0.0 copy-start
  63.4 10.3 %all-to-all-start = ((bf16[32,8,2560]{2,1,0:T(8,128)(2,1)}), bf16[32,8,2560]{2,1,0:T(8,128)(2,1)}, u32[]{:S(2)}, u32[]{:S(2)}) async-start(bf16[32,8,2560]{2,1,0:T(8,128)(2,1)} %bitcast.24), calls=%async_computation | async-start | bytes 2621440 | tf_op jit(solution)/shard_map/all_to_all | solution.py:520
  73.7 0.0 collective-permute-done.5.refs_1_
  73.7 0.0 copy-done
  73.7 1.0 shard_map.146.refs_0_
  74.7 0.0 copy-start.3
  74.7 2.5 %collective-permute-start.8 = (bf16[256,1152]{1,0:T(8,128)(2,1)S(1)}, bf16[256,1152]{1,0:T(8,128)(2,1)S(1)}, u32[]{:S(2)}, u32[]{:S(2)}) collective-permute-start(bf16[256,1152]{1,0:T(8,128)(2,1)S(1)} %shard_map.146.refs_0_), channel_id=1, source_target_pairs={{0,384},{32,416},{64,448},{96,480},{128,0},{160,32},{192,64},{224,... | collective-permute-start | bytes 1769480 | tf_op jit(solution)/shard_map/ppermute | solution.py:455
  77.2 3.4 %collective-permute-start.6 = (bf16[256,1152]{1,0:T(8,128)(2,1)S(1)}, bf16[256,1152]{1,0:T(8,128)(2,1)S(1)}, u32[]{:S(2)}, u32[]{:S(2)}) collective-permute-start(bf16[256,1152]{1,0:T(8,128)(2,1)S(1)} %shard_map.146.refs_0_), channel_id=1, source_target_pairs={{0,128},{32,160},{64,192},{96,224},{128,256},{160,288},{192,320},{... | collective-permute-start | bytes 1769480 | tf_op jit(solution)/shard_map/ppermute | solution.py:455
  80.6 1.9 collective-permute-start.10
  82.5 9.0 %collective-permute-done.8.refs_4_ = bf16[256,1152]{1,0:T(8,128)(2,1)S(1)} collective-permute-done((bf16[256,1152]{1,0:T(8,128)(2,1)S(1)}, bf16[256,1152]{1,0:T(8,128)(2,1)S(1)}, u32[]{:S(2)}, u32[]{:S(2)}) %collective-permute-start.8) | collective-permute-done | bytes 589856 | tf_op jit(solution)/shard_map/ppermute | solution.py:455
  91.5 3.7 %collective-permute-start.9 = (bf16[128,1152]{1,0:T(8,128)(2,1)S(1)}, bf16[128,1152]{1,0:T(8,128)(2,1)S(1)}, u32[]{:S(2)}, u32[]{:S(2)}) collective-permute-start(bf16[128,1152]{1,0:T(8,128)(2,1)S(1)} %slice.9), channel_id=1, source_target_pairs={{0,384},{32,416},{64,448},{96,480},{128,0},{160,32},{192,64},{224,... | collective-permute-start | bytes 884744 | tf_op jit(solution)/shard_map/ppermute | solution.py:455
  95.2 0.0 collective-permute-done.6.refs_1_
  95.2 0.0 copy-start.5
  95.3 2.2 %collective-permute-start.7 = (bf16[128,1152]{1,0:T(8,128)(2,1)S(1)}, bf16[128,1152]{1,0:T(8,128)(2,1)S(1)}, u32[]{:S(2)}, u32[]{:S(2)}) collective-permute-start(bf16[128,1152]{1,0:T(8,128)(2,1)S(1)} %slice.8), channel_id=1, source_target_pairs={{0,128},{32,160},{64,192},{96,224},{128,256},{160,288},{192,320},{... | collective-permute-start | bytes 884744 | tf_op jit(solution)/shard_map/ppermute | solution.py:455
  97.4 1.9 collective-permute-start.14
  99.4 2.4 %collective-permute-start.11 = (bf16[256,1152]{1,0:T(8,128)(2,1)S(1)}, bf16[256,1152]{1,0:T(8,128)(2,1)S(1)}, u32[]{:S(2)}, u32[]{:S(2)}) collective-permute-start(bf16[256,1152]{1,0:T(8,128)(2,1)S(1)} %collective-permute-done.6.refs_1_), channel_id=1, source_target_pairs={{0,32},{32,0},{64,96},{96,64},{128,160},{160,128},{192,224},{224,1... | collective-permute-start | bytes 1769480 | tf_op jit(solution)/shard_map/ppermute | solution.py:455
  101.8 0.0 collective-permute-done.9.refs_3_
  101.8 0.0 copy-start.10
  101.8 2.1 %collective-permute-start.13 = (bf16[128,1152]{1,0:T(8,128)(2,1)S(1)}, bf16[128,1152]{1,0:T(8,128)(2,1)S(1)}, u32[]{:S(2)}, u32[]{:S(2)}) collective-permute-start(bf16[128,1152]{1,0:T(8,128)(2,1)S(1)} %collective-permute-done.9.refs_3_), channel_id=1, source_target_pairs={{0,32},{32,0},{64,96},{96,64},{128,160},{160,128},{192,224},{224,1... | collective-permute-start | bytes 884744 | tf_op jit(solution)/shard_map/ppermute | solution.py:455
  103.9 2.0 collective-permute-done.7.refs_2_
  105.9 1.9 collective-permute-start.12
  107.8 0.0 collective-permute-done.10.refs_5_
  107.8 0.0 copy-start.7
  107.8 0.0 collective-permute-done.13.refs_8_
  107.8 0.0 copy-start.12
  107.8 1.5 collective-permute-done.12.refs_7_
  109.3 0.0 collective-permute-done.14.refs_9_
  109.3 0.0 copy-done.10
  109.4 0.0 copy-done.11
  109.4 0.0 copy-done.12
  109.4 0.7 copy-done.13
  110.1 0.0 collective-permute-done.11.refs_6_
  110.1 0.0 all-to-all-done
  110.1 0.0 copy-done.3
  110.1 0.8 copy-done.8
  110.9 0.2 copy-done.9
  111.1 9.7 %shard_map.147 = bf16[256,5120]{1,0:T(8,128)(2,1)} custom-call(s32[1]{0:T(128)} %bitcast.me_ref, bf16[256,2560]{1,0:T(8,128)(2,1)} %bitcast.14.rows_hbm, bf16[256,2560]{1,0:T(8,128)(2,1)} %bitcast.18.grads_hbm, bf16[256,1152]{1,0:T(8,128)(2,1)} %copy-done.3, bf16[256,1152]{1,0:T(8,128)(2,1)} %copy-done.5, bf16[128,1152]{1,0:T(8,128)(2,1)} %copy-done.11, ...), custom_call_target="tpu_custom_call" | custom-call | flops 3019898880 | bytes 10485760 | tf_op jit(solution)/shard_map/pallas_call | solution.py:554
  120.8 72.0 %all_to_all.15 = bf16[32,8,5120]{2,1,0:T(8,128)(2,1)} all-to-all(bf16[32,8,5120]{2,1,0:T(8,128)(2,1)} %bitcast.27), channel_id=1, replica_groups=mesh['ctx'=16,'exp'=32] {'exp'}, dimensions={0} | all-to-all | bytes 5242880 | tf_op jit(solution)/shard_map/all_to_all | solution.py:520
  192.8 4.7 %shard_map.148 = (bf16[128,2048]{1,0:T(8,128)(2,1)}, f32[128,2048]{1,0:T(8,128)}) custom-call(bf16[256,5120]{1,0:T(8,128)(2,1)} %bitcast.25, f32[128,2048]{1,0:T(8,128)} %get-tuple-element.12.stream_hbm, bf16[128,2048]{1,0:T(8,128)(2,1)} %bitcast.29, f32[1,2048]{1,0:T(1,128)} %bitcast.39, bf16[128,2560]{1,0:T(8,128)(2,1)} %get-tuple-element.13.factor_hbm), custom_call_target="tpu_custom_call" | custom-call | tf_op jit(solution)/shard_map/pallas_call | solution.py:574
  (10 shorter events, 0.1 us)
Async XLA Ops:
  2.2 21.3 %collective-permute-start = (bf16[128,512]{1,0:T(8,128)(2,1)}, bf16[128,512]{1,0:T(8,128)(2,1)S(1)}, u32[]{:S(2)}, u32[]{:S(2)}) collective-permute-start(bf16[128,512]{1,0:T(8,128)(2,1)} %shard_map.140.refs_0_), channel_id=1, source_target_pairs={{0,64},{32,96},{64,0},{96,32},{128,192},{160,224},{192,128},{224,1... | collective-permute-start | bytes 393224 | tf_op jit(solution)/shard_map/ppermute | solution.py:455
  9.6 14.0 %copy-start.2 = (bf16[128,512]{1,0:T(8,128)(2,1)S(1)}, bf16[128,512]{1,0:T(8,128)(2,1)}, u32[]{:S(2)}) copy-start(bf16[128,512]{1,0:T(8,128)(2,1)} %shard_map.140.refs_0_) | copy-start | bytes 393220
  9.6 53.8 %all-to-all-start.1 = ((bf16[32,8,2560]{2,1,0:T(8,128)(2,1)}), bf16[32,8,2560]{2,1,0:T(8,128)(2,1)}, u32[]{:S(2)}, u32[]{:S(2)}) async-start(bf16[32,8,2560]{2,1,0:T(8,128)(2,1)} %bitcast.26), calls=%async_computation.1 | async-start | bytes 2621440 | tf_op jit(solution)/shard_map/all_to_all | solution.py:520
  23.9 15.6 %collective-permute-start.3 = (bf16[256,512]{1,0:T(8,128)(2,1)S(1)}, bf16[256,512]{1,0:T(8,128)(2,1)S(1)}, u32[]{:S(2)}, u32[]{:S(2)}) collective-permute-start(bf16[256,512]{1,0:T(8,128)(2,1)S(1)} %shard_map.141.refs_0_), channel_id=1, source_target_pairs={{0,384},{32,416},{64,448},{96,480},{128,0},{160,32},{192,64},{224,... | collective-permute-start | bytes 786440 | tf_op jit(solution)/shard_map/ppermute | solution.py:455
  28.6 12.6 %collective-permute-start.2 = (bf16[256,512]{1,0:T(8,128)(2,1)S(1)}, bf16[256,512]{1,0:T(8,128)(2,1)S(1)}, u32[]{:S(2)}, u32[]{:S(2)}) collective-permute-start(bf16[256,512]{1,0:T(8,128)(2,1)S(1)} %shard_map.141.refs_0_), channel_id=1, source_target_pairs={{0,256},{32,288},{64,320},{96,352},{128,384},{160,416},{192,448},{... | collective-permute-start | bytes 786440 | tf_op jit(solution)/shard_map/ppermute | solution.py:455
  31.3 13.2 %collective-permute-start.1 = (bf16[256,512]{1,0:T(8,128)(2,1)S(1)}, bf16[256,512]{1,0:T(8,128)(2,1)S(1)}, u32[]{:S(2)}, u32[]{:S(2)}) collective-permute-start(bf16[256,512]{1,0:T(8,128)(2,1)S(1)} %shard_map.141.refs_0_), channel_id=1, source_target_pairs={{0,128},{32,160},{64,192},{96,224},{128,256},{160,288},{192,320},{... | collective-permute-start | bytes 786440 | tf_op jit(solution)/shard_map/ppermute | solution.py:455
  44.6 8.0 %copy-start.1 = (bf16[1024,512]{1,0:T(8,128)(2,1)}, bf16[1024,512]{1,0:T(8,128)(2,1)S(1)}, u32[]{:S(2)}) copy-start(bf16[1024,512]{1,0:T(8,128)(2,1)S(1)} %shard_map.143.mine_hbm) | copy-start | bytes 3145732
  44.6 7.0 %collective-permute-start.4 = (bf16[1024,512]{1,0:T(8,128)(2,1)S(1)}, bf16[1024,512]{1,0:T(8,128)(2,1)S(1)}, u32[]{:S(2)}, u32[]{:S(2)}) collective-permute-start(bf16[1024,512]{1,0:T(8,128)(2,1)S(1)} %shard_map.143.mine_hbm), channel_id=1, source_target_pairs={{0,32},{32,0},{64,96},{96,64},{128,160},{160,128},{192,224},{224,1... | collective-permute-start | bytes 3145736 | tf_op jit(solution)/shard_map/ppermute | solution.py:455
  46.6 27.1 %collective-permute-start.5 = (bf16[128,1152]{1,0:T(8,128)(2,1)}, bf16[128,1152]{1,0:T(8,128)(2,1)S(1)}, u32[]{:S(2)}, u32[]{:S(2)}) collective-permute-start(bf16[128,1152]{1,0:T(8,128)(2,1)} %get-tuple-element.9.refs_4_.refs_0_), channel_id=1, source_target_pairs={{0,64},{32,96},{64,0},{96,32},{128,192},{160,224},{192,128},{224,1... | collective-permute-start | bytes 884744 | tf_op jit(solution)/shard_map/ppermute | solution.py:455
  51.6 1.0 copy-start.6
  63.4 10.3 %copy-start = (bf16[256,2560]{1,0:T(8,128)(2,1)S(1)}, bf16[256,2560]{1,0:T(8,128)(2,1)}, u32[]{:S(2)}) copy-start(bf16[256,2560]{1,0:T(8,128)(2,1)} %get-tuple-element.11.refs_2_) | copy-start | bytes 3932164
  63.4 46.6 %all-to-all-start = ((bf16[32,8,2560]{2,1,0:T(8,128)(2,1)}), bf16[32,8,2560]{2,1,0:T(8,128)(2,1)}, u32[]{:S(2)}, u32[]{:S(2)}) async-start(bf16[32,8,2560]{2,1,0:T(8,128)(2,1)} %bitcast.24), calls=%async_computation | async-start | bytes 2621440 | tf_op jit(solution)/shard_map/all_to_all | solution.py:520
  74.7 35.4 %copy-start.3 = (bf16[256,1152]{1,0:T(8,128)(2,1)}, bf16[256,1152]{1,0:T(8,128)(2,1)S(1)}, u32[]{:S(2)}) copy-start(bf16[256,1152]{1,0:T(8,128)(2,1)S(1)} %shard_map.146.refs_0_) | copy-start | bytes 1769476
  74.7 16.8 %collective-permute-start.8 = (bf16[256,1152]{1,0:T(8,128)(2,1)S(1)}, bf16[256,1152]{1,0:T(8,128)(2,1)S(1)}, u32[]{:S(2)}, u32[]{:S(2)}) collective-permute-start(bf16[256,1152]{1,0:T(8,128)(2,1)S(1)} %shard_map.146.refs_0_), channel_id=1, source_target_pairs={{0,384},{32,416},{64,448},{96,480},{128,0},{160,32},{192,64},{224,... | collective-permute-start | bytes 1769480 | tf_op jit(solution)/shard_map/ppermute | solution.py:455
  77.2 18.0 %collective-permute-start.6 = (bf16[256,1152]{1,0:T(8,128)(2,1)S(1)}, bf16[256,1152]{1,0:T(8,128)(2,1)S(1)}, u32[]{:S(2)}, u32[]{:S(2)}) collective-permute-start(bf16[256,1152]{1,0:T(8,128)(2,1)S(1)} %shard_map.146.refs_0_), channel_id=1, source_target_pairs={{0,128},{32,160},{64,192},{96,224},{128,256},{160,288},{192,320},{... | collective-permute-start | bytes 1769480 | tf_op jit(solution)/shard_map/ppermute | solution.py:455
  80.6 27.2 %collective-permute-start.10 = (bf16[256,1152]{1,0:T(8,128)(2,1)S(1)}, bf16[256,1152]{1,0:T(8,128)(2,1)S(1)}, u32[]{:S(2)}, u32[]{:S(2)}) collective-permute-start(bf16[256,1152]{1,0:T(8,128)(2,1)S(1)} %shard_map.146.refs_0_), channel_id=1, source_target_pairs={{0,32},{32,0},{64,96},{96,64},{128,160},{160,128},{192,224},{224,1... | collective-permute-start | bytes 1769480 | tf_op jit(solution)/shard_map/ppermute | solution.py:455
  91.5 18.6 %copy-start.4 = (bf16[256,1152]{1,0:T(8,128)(2,1)}, bf16[256,1152]{1,0:T(8,128)(2,1)S(1)}, u32[]{:S(2)}) copy-start(bf16[256,1152]{1,0:T(8,128)(2,1)S(1)} %collective-permute-done.8.refs_4_) | copy-start | bytes 1769476
  91.5 10.3 %collective-permute-start.9 = (bf16[128,1152]{1,0:T(8,128)(2,1)S(1)}, bf16[128,1152]{1,0:T(8,128)(2,1)S(1)}, u32[]{:S(2)}, u32[]{:S(2)}) collective-permute-start(bf16[128,1152]{1,0:T(8,128)(2,1)S(1)} %slice.9), channel_id=1, source_target_pairs={{0,384},{32,416},{64,448},{96,480},{128,0},{160,32},{192,64},{224,... | collective-permute-start | bytes 884744 | tf_op jit(solution)/shard_map/ppermute | solution.py:455
  95.2 14.9 %copy-start.5 = (bf16[256,1152]{1,0:T(8,128)(2,1)}, bf16[256,1152]{1,0:T(8,128)(2,1)S(1)}, u32[]{:S(2)}) copy-start(bf16[256,1152]{1,0:T(8,128)(2,1)S(1)} %collective-permute-done.6.refs_1_) | copy-start | bytes 1769476
  95.3 10.6 %collective-permute-start.7 = (bf16[128,1152]{1,0:T(8,128)(2,1)S(1)}, bf16[128,1152]{1,0:T(8,128)(2,1)S(1)}, u32[]{:S(2)}, u32[]{:S(2)}) collective-permute-start(bf16[128,1152]{1,0:T(8,128)(2,1)S(1)} %slice.8), channel_id=1, source_target_pairs={{0,128},{32,160},{64,192},{96,224},{128,256},{160,288},{192,320},{... | collective-permute-start | bytes 884744 | tf_op jit(solution)/shard_map/ppermute | solution.py:455
  97.4 11.9 %collective-permute-start.14 = (bf16[256,1152]{1,0:T(8,128)(2,1)S(1)}, bf16[256,1152]{1,0:T(8,128)(2,1)S(1)}, u32[]{:S(2)}, u32[]{:S(2)}) collective-permute-start(bf16[256,1152]{1,0:T(8,128)(2,1)S(1)} %collective-permute-done.8.refs_4_), channel_id=1, source_target_pairs={{0,32},{32,0},{64,96},{96,64},{128,160},{160,128},{192,224},{224,1... | collective-permute-start | bytes 1769480 | tf_op jit(solution)/shard_map/ppermute | solution.py:455
  99.4 10.7 %collective-permute-start.11 = (bf16[256,1152]{1,0:T(8,128)(2,1)S(1)}, bf16[256,1152]{1,0:T(8,128)(2,1)S(1)}, u32[]{:S(2)}, u32[]{:S(2)}) collective-permute-start(bf16[256,1152]{1,0:T(8,128)(2,1)S(1)} %collective-permute-done.6.refs_1_), channel_id=1, source_target_pairs={{0,32},{32,0},{64,96},{96,64},{128,160},{160,128},{192,224},{224,1... | collective-permute-start | bytes 1769480 | tf_op jit(solution)/shard_map/ppermute | solution.py:455
  101.8 7.5 %copy-start.10 = (bf16[128,1152]{1,0:T(8,128)(2,1)}, bf16[128,1152]{1,0:T(8,128)(2,1)S(1)}, u32[]{:S(2)}) copy-start(bf16[128,1152]{1,0:T(8,128)(2,1)S(1)} %collective-permute-done.9.refs_3_) | copy-start | bytes 884740
  101.8 6.0 %collective-permute-start.13 = (bf16[128,1152]{1,0:T(8,128)(2,1)S(1)}, bf16[128,1152]{1,0:T(8,128)(2,1)S(1)}, u32[]{:S(2)}, u32[]{:S(2)}) collective-permute-start(bf16[128,1152]{1,0:T(8,128)(2,1)S(1)} %collective-permute-done.9.refs_3_), channel_id=1, source_target_pairs={{0,32},{32,0},{64,96},{96,64},{128,160},{160,128},{192,224},{224,1... | collective-permute-start | bytes 884744 | tf_op jit(solution)/shard_map/ppermute | solution.py:455
  105.9 3.5 %copy-start.11 = (bf16[128,1152]{1,0:T(8,128)(2,1)}, bf16[128,1152]{1,0:T(8,128)(2,1)S(1)}, u32[]{:S(2)}) copy-start(bf16[128,1152]{1,0:T(8,128)(2,1)S(1)} %collective-permute-done.7.refs_2_) | copy-start | bytes 884740
  105.9 3.5 %collective-permute-start.12 = (bf16[128,1152]{1,0:T(8,128)(2,1)S(1)}, bf16[128,1152]{1,0:T(8,128)(2,1)S(1)}, u32[]{:S(2)}, u32[]{:S(2)}) collective-permute-start(bf16[128,1152]{1,0:T(8,128)(2,1)S(1)} %collective-permute-done.7.refs_2_), channel_id=1, source_target_pairs={{0,32},{32,0},{64,96},{96,64},{128,160},{160,128},{192,224},{224,1... | collective-permute-start | bytes 884744 | tf_op jit(solution)/shard_map/ppermute | solution.py:455
  107.8 2.3 %copy-start.7 = (bf16[256,1152]{1,0:T(8,128)(2,1)}, bf16[256,1152]{1,0:T(8,128)(2,1)S(1)}, u32[]{:S(2)}) copy-start(bf16[256,1152]{1,0:T(8,128)(2,1)S(1)} %collective-permute-done.10.refs_5_) | copy-start | bytes 1769476
  107.8 1.5 copy-start.12
  109.3 0.7 copy-start.13
  110.1 0.8 copy-start.8
  110.1 1.0 copy-start.9
